TPU v7x, 128 devices: a whole 4x4x4 slice. The times are simulated.
128 devices in a mesh: lon: 16 (over z, x_lo, core), lat: 8 (over y, x_hi).
Axes of the slice: x: 4 (x_hi: 2, x_lo: 2; x = x_hi * 2 + x_lo), y: 4, z: 4, core: 2. Of those that a mesh axis runs over, the one named last changes fastest.
Arguments:
- tokens: bfloat16 [96, 384, 4, 512], P('lat', 'lon'), may hold values from -6 to 6
- surface_kind: int32 [96, 384], P('lat', 'lon'), may hold values from 0 to 2
- kind_table: bfloat16 [3, 4, 512], replicated, may hold values from -3 to 3
- attn_q_w: bfloat16 [512, 512], replicated, as said below
- attn_kv_w: bfloat16 [512, 1024], replicated, as said below
- attn_out_w: bfloat16 [512, 512], replicated, may hold values from -0.25 to 0.25
- mlp_in_w: bfloat16 [512, 2048], replicated, may hold values from -0.25 to 0.25
- mlp_out_w: bfloat16 [2048, 512], replicated, may hold values from -0.125 to 0.125
- merge_w: bfloat16 [2048, 1024], replicated, may hold values from -0.125 to 0.125
- coarse_qkv_w: bfloat16 [1024, 3072], replicated
- coarse_out_w: bfloat16 [1024, 1024], replicated, may hold values from -0.1875 to 0.1875
Outputs:
- fine_state: bfloat16 [96, 384, 4, 512], P('lat', 'lon')
- coarse_state: bfloat16 [48, 192, 4, 1024], P('lat', 'lon')
Inputs may be any that keep to these rules, and one draw needn't show every extreme that they name: `attn_q_w`: a projection of 512 inputs. `attn_kv_w`: a projection of 512 inputs.
All inputs are finite; a program needn't handle non-finite values.
Results may differ from a plain program's by a relative error of at most 0.02.
Values may be sent and summed in bfloat16 or wider, within the bound.
A program may use at most 128 MiB of HBM per device.

v0:
```python
import jax
import jax.numpy as jnp
from jax import lax
from jax.sharding import PartitionSpec as P

H1 = 8
H2 = 16


epsilon = 1e-05


def with_halo(cells, sides, width):
    for axis, dim in sides:
        count = lax.axis_size(axis)
        head = lax.slice_in_dim(cells, 0, width, axis=dim)
        tail = lax.slice_in_dim(cells, cells.shape[dim] - width, cells.shape[dim], axis=dim)
        cells = jnp.concatenate(
            [
                lax.ppermute(tail, axis, [(i, (i + 1) % count) for i in range(count)]),
                cells,
                lax.ppermute(head, axis, [((i + 1) % count, i) for i in range(count)]),
            ],
            axis=dim,
        )
    return cells


def normalize(tensor):
    tensor = tensor.astype(jnp.float32)
    centred = tensor - jnp.mean(tensor, axis=-1, keepdims=True)
    spread = jnp.mean(centred * centred, axis=-1, keepdims=True)
    return (centred * lax.rsqrt(spread + epsilon)).astype(jnp.bfloat16)


def to_windows(tensor):
    full_shape = tensor.shape
    row_count = full_shape[0]
    col_count = full_shape[1]
    levels = full_shape[2]
    tail_dims = tuple(full_shape[3:])
    tensor = tensor.reshape((row_count // 6, 6, col_count // 12, 12) + tuple(full_shape[2:]))
    axis_order = (0, 2, 1, 3) + tuple(range(4, 4 + len(full_shape) - 2))
    tensor = tensor.transpose(axis_order)
    return tensor.reshape((row_count // 6, col_count // 12, 72 * levels) + tail_dims)


def from_windows(tensor, levels):
    win_rows, win_cols, tokens_win, feat_width = tensor.shape
    tensor = tensor.reshape(win_rows, win_cols, 6, 12, levels, feat_width).transpose(
        0, 2, 1, 3, 4, 5
    )
    return tensor.reshape(win_rows * 6, win_cols * 12, levels, feat_width)


def window_attention(query_win, pair_win, valid_win, head_count, levels):
    win_rows, win_cols, tokens_win, feat_width = query_win.shape
    head_size = feat_width // head_count
    score_scale = head_size ** (-0.5)
    level_group = (jnp.arange(tokens_win) % levels + 1) // 2
    same_group = level_group[:, None] == level_group[None, :]

    def window_row(pieces):
        query_row, pair_row, valid_row = pieces
        query_heads = query_row.reshape(win_cols, tokens_win, head_count, head_size)
        key_heads = pair_row[:, :, 0].reshape(win_cols, tokens_win, head_count, head_size)
        value_heads = pair_row[:, :, 1].reshape(win_cols, tokens_win, head_count, head_size)
        scores = (
            jnp.einsum(
                "nqhd,nkhd->nhqk", query_heads, key_heads, preferred_element_type=jnp.float32
            )
            * score_scale
        )
        allowed = (valid_row[:, None, None, :] > 0.5) & same_group[None, None]
        scores = jnp.where(allowed, scores, -1e30)
        row_top = jnp.max(scores, axis=-1, keepdims=True)
        weights = jnp.exp(scores - row_top)
        weights_bf = (weights / jnp.sum(weights, axis=-1, keepdims=True)).astype(jnp.bfloat16)
        mixture = jnp.einsum(
            "nhqk,nkhd->nqhd", weights_bf, value_heads, preferred_element_type=jnp.float32
        )
        return mixture.reshape(win_cols, tokens_win, feat_width).astype(jnp.bfloat16)

    return lax.map(window_row, (query_win, pair_win, valid_win))


def merge_patches(grid_state):
    lat_rows, lon_cols, levels, feat_width = grid_state.shape
    grid_state = grid_state.reshape(lat_rows // 2, 2, lon_cols // 2, 2, levels, feat_width)
    grid_state = grid_state.transpose(0, 2, 4, 3, 1, 5)
    return grid_state.reshape(lat_rows // 2, lon_cols // 2, levels, 4 * feat_width)


def local(
    tokens,
    surface_kind,
    kind_table,
    attn_q_w,
    attn_kv_w,
    attn_out_w,
    mlp_in_w,
    mlp_out_w,
    merge_w,
    coarse_qkv_w,
    coarse_out_w,
):
    lat_rows, lon_cols, levels, feat_width = tokens.shape
    kind_count = kind_table.shape[0]
    onehot = (
        surface_kind.reshape(lat_rows * lon_cols, 1) == jnp.arange(kind_count)[None, :]
    ).astype(jnp.bfloat16)
    kind_embed = jnp.dot(
        onehot,
        kind_table.reshape(kind_count, levels * feat_width),
        preferred_element_type=jnp.float32,
    )
    embedded = (
        tokens.astype(jnp.float32) + kind_embed.reshape(lat_rows, lon_cols, levels, feat_width)
    ).astype(jnp.bfloat16)
    framed = with_halo(embedded, (("lon", 1), ("lat", 0)), 6)[3:-3]
    frame_rows = framed.shape[0]
    frame_cols = framed.shape[1]
    normed_win = to_windows(normalize(framed))
    win_rows, win_cols, tokens_win = (normed_win.shape[0], normed_win.shape[1], normed_win.shape[2])
    query_win = jnp.dot(normed_win, attn_q_w, preferred_element_type=jnp.float32).astype(
        jnp.bfloat16
    )
    pair_win = jnp.dot(normed_win, attn_kv_w, preferred_element_type=jnp.float32).astype(
        jnp.bfloat16
    )
    pair_win = pair_win.reshape(win_rows, win_cols, tokens_win, 2, feat_width)
    lat_start = lax.axis_index("lat") * lat_rows - 3
    lat_place = lat_start + jnp.arange(frame_rows)
    lat_inside = ((lat_place >= 0) & (lat_place < lat_rows * lax.axis_size("lat"))).astype(
        jnp.float32
    )
    valid_grid = jnp.broadcast_to(
        lat_inside[:, None, None, None], (frame_rows, frame_cols, levels, 1)
    )
    valid_win = to_windows(valid_grid)[..., 0]
    attended_win = window_attention(query_win, pair_win, valid_win, H1, levels)
    attended = from_windows(attended_win, levels)[3 : 3 + lat_rows, 6 : 6 + lon_cols]
    after_attn = (
        embedded.astype(jnp.float32)
        + jnp.dot(attended, attn_out_w, preferred_element_type=jnp.float32)
    ).astype(jnp.bfloat16)
    hidden = jax.nn.gelu(
        jnp.dot(normalize(after_attn), mlp_in_w, preferred_element_type=jnp.float32)
    ).astype(jnp.bfloat16)
    fine_state = (
        after_attn.astype(jnp.float32)
        + jnp.dot(hidden, mlp_out_w, preferred_element_type=jnp.float32)
    ).astype(jnp.bfloat16)
    merged = merge_patches(fine_state)
    coarse_in = jnp.dot(normalize(merged), merge_w, preferred_element_type=jnp.float32).astype(
        jnp.bfloat16
    )
    coarse_width = coarse_in.shape[-1]
    band_rows = lat_rows // 2
    band_cols = lon_cols // 2
    normed_coarse = normalize(coarse_in)
    coarse_query = jnp.dot(
        normed_coarse, coarse_qkv_w[:, :coarse_width], preferred_element_type=jnp.float32
    ).astype(jnp.bfloat16)
    coarse_query = coarse_query.reshape(band_rows, band_cols, levels, 1, coarse_width)
    coarse_pair = jnp.dot(
        normed_coarse, coarse_qkv_w[:, coarse_width:], preferred_element_type=jnp.float32
    ).astype(jnp.bfloat16)
    coarse_pair = coarse_pair.reshape(band_rows, band_cols, levels, 2, coarse_width)
    relaid_query, relaid_pair = (
        lax.all_to_all(coarse_query, "lat", split_axis=4, concat_axis=0, tiled=True),
        lax.all_to_all(coarse_pair, "lat", split_axis=4, concat_axis=0, tiled=True),
    )
    all_rows = relaid_query.shape[0]
    own_width = relaid_query.shape[-1]
    wide_pair = with_halo(relaid_pair, (("lon", 1),), 6)
    wide_pair = jnp.pad(wide_pair, ((3, 3), (0, 0), (0, 0), (0, 0), (0, 0)))
    query_frame = jnp.pad(relaid_query[:, :, :, 0], ((3, 3), (6, 6), (0, 0), (0, 0)))
    coarse_valid = jnp.pad(
        jnp.ones((all_rows, band_cols + 12, levels, 1), jnp.float32),
        ((3, 3), (0, 0), (0, 0), (0, 0)),
    )
    coarse_win = window_attention(
        to_windows(query_frame),
        to_windows(wide_pair),
        to_windows(coarse_valid)[..., 0],
        H2 // lax.axis_size("lat"),
        levels,
    )
    coarse_mix = from_windows(coarse_win, levels)[3 : 3 + all_rows, 6 : 6 + band_cols]
    own_weight = lax.dynamic_slice_in_dim(
        coarse_out_w, lax.axis_index("lat") * own_width, own_width, 0
    )
    projected = lax.psum_scatter(
        jnp.dot(coarse_mix, own_weight, preferred_element_type=jnp.float32).astype(jnp.bfloat16),
        "lat",
        scatter_dimension=0,
        tiled=True,
    ).astype(jnp.float32)
    coarse_state = (coarse_in.astype(jnp.float32) + projected).astype(jnp.bfloat16)
    return (fine_state, coarse_state)


def solution(mesh):
    in_specs = (
        P("lat", "lon", None, None),
        P("lat", "lon"),
        P(),
        P(),
        P(),
        P(),
        P(),
        P(),
        P(),
        P(),
        P(),
    )
    out_specs = (P("lat", "lon", None, None), P("lat", "lon", None, None))
    return jax.shard_map(local, mesh=mesh, in_specs=in_specs, out_specs=out_specs, check_vma=False)
```

profile of v0, /device:TPU:0, one launch (start us, length us, event | category | flops | bytes accessed | tf_op | source)
XLA Modules:
  0.0 754.6 jit_solution(7442103084080323062)
XLA Ops:
  9.5 4.6 collective-permute-start.1
  14.0 6.9 collective-permute-done
  29.2 3.4 collective-permute-start.3
  32.9 18.6 %collective-permute-done.2 = bf16[6,36,4,512]{3,2,1,0:T(4,128)(2,1)} collective-permute-done((bf16[6,36,4,512]{3,2,1,0:T(4,128)(2,1)}, bf16[6,36,4,512]{3,2,1,0:T(4,128)(2,1)}, u32[]{:S(2)}, u32[]{:S(2)}) %collective-permute-start.2) | collective-permute-done | bytes 884768 | tf_op jit(solution)/shard_map/ppermute | solution.py:20
  52.8 16.1 %collective-permute-done.3 = bf16[6,36,4,512]{3,2,1,0:T(4,128)(2,1)} collective-permute-done((bf16[6,36,4,512]{3,2,1,0:T(4,128)(2,1)}, bf16[6,36,4,512]{3,2,1,0:T(4,128)(2,1)}, u32[]{:S(2)}, u32[]{:S(2)}) %collective-permute-start.3) | collective-permute-done | bytes 884768 | tf_op jit(solution)/shard_map/ppermute | solution.py:22
  78.2 5.4 reshape.267
  83.6 6.5 convolution_convert_fusion.1
  90.1 13.0 %reshape.268 = bf16[3,3,288,2,512]{4,3,2,1,0:T(2,128)(2,1)} reshape(bf16[3,3,288,1024]{3,2,1,0:T(8,128)(2,1)} %convolution_convert_fusion.1) | data formatting | bytes 10616832 | tf_op jit(solution)/shard_map/reshape | solution.py:131
  103.1 4.8 convolution_convert_fusion.3
  107.9 103.2 %while.22 = (s32[]{:T(128)}, bf16[3,3,288,512]{3,2,1,0:T(8,128)(2,1)}, bf16[3,3,288,2,512]{4,3,2,1,0:T(2,128)(2,1)}, f32[3,3,288]{2,1,0:T(4,128)S(1)}, bf16[3,3,...) while((s32[]{:T(128)}, bf16[3,3,288,512]{3,2,1,0:T(8,128)(2,1)}, ...), condition=%wide.region_5.6_spmd.clone, body=%wide.region_2.5_spmd.clone.sunk | while | flops 522327168 | bytes 41423668 | solution.py:84
  108.0 3.9 constant_dynamic-slice_fusion.9
  111.9 5.2 copy.305
  117.2 3.3 fusion.151
  124.1 9.5 %fusion.153 = (f32[3,8,288]{2,1,0:T(8,128)S(1)}, f32[3,8,288,288]{2,3,1,0:T(8,128)}) fusion(pred[3,288,288]{1,2,0:T(8,128)(4,1)} %broadcast_and_fusion.4, bf16[3,288,8,64]{1,3,2,0:T(8,128)(2,1)} %bitcast.195, bf16[3,288,8,64]{1,3,2,0:T(8,128)(2,1)} %bitcast.198), kind=kOutput, calls=%fused_computation.150.clone.1 | convolution fusion | flops 262766880 | bytes 10008576 | tf_op jit(solution)/shard_map/while/body/eval_jaxpr/sub | solution.py:77
  133.6 6.3 fusion.154
  142.4 3.9 constant_dynamic-slice_fusion.9
  146.3 5.2 copy.305
  151.5 3.3 fusion.151
  158.5 9.5 %fusion.153 = (f32[3,8,288]{2,1,0:T(8,128)S(1)}, f32[3,8,288,288]{2,3,1,0:T(8,128)}) fusion(pred[3,288,288]{1,2,0:T(8,128)(4,1)} %broadcast_and_fusion.4, bf16[3,288,8,64]{1,3,2,0:T(8,128)(2,1)} %bitcast.195, bf16[3,288,8,64]{1,3,2,0:T(8,128)(2,1)} %bitcast.198), kind=kOutput, calls=%fused_computation.150.clone.1 | convolution fusion | flops 262766880 | bytes 10008576 | tf_op jit(solution)/shard_map/while/body/eval_jaxpr/sub | solution.py:77
  168.0 6.3 fusion.154
  176.8 3.9 constant_dynamic-slice_fusion.9
  180.7 5.2 copy.305
  192.9 9.5 %fusion.153 = (f32[3,8,288]{2,1,0:T(8,128)S(1)}, f32[3,8,288,288]{2,3,1,0:T(8,128)}) fusion(pred[3,288,288]{1,2,0:T(8,128)(4,1)} %broadcast_and_fusion.4, bf16[3,288,8,64]{1,3,2,0:T(8,128)(2,1)} %bitcast.195, bf16[3,288,8,64]{1,3,2,0:T(8,128)(2,1)} %bitcast.198), kind=kOutput, calls=%fused_computation.150.clone.1 | convolution fusion | flops 262766880 | bytes 10008576 | tf_op jit(solution)/shard_map/while/body/eval_jaxpr/sub | solution.py:77
  202.3 6.3 fusion.154
  211.1 5.8 reshape.269
  223.2 9.2 %fusion.51 = bf16[12,24,4,512]{3,1,2,0:T(8,128)(2,1)S(1)} fusion(bf16[12,24,4,512]{3,1,2,0:T(8,128)(2,1)} %copy-done.13, bf16[2048,512]{1,0:T(8,128)(2,1)} %param.22, bf16[512,2048]{1,0:T(8,128)(2,1)} %param.21, f32[12,24,4]{1,2,0:T(4,128)S(1)} %add_rsqrt_fusion.2, f32[12,24,4]{1,2,0:T(4,128)S(1)} %broadcast_multiply_fusion.2), kind=kOutput, calls=%fused_computation.81 | convolution fusion | flops 4857200640 | bytes 6562816 | tf_op jit(solution)/shard_map/dot_general | solution.py:152
  235.3 3.9 fusion.116
  239.1 3.3 copy.298
  244.8 4.5 reshape.279
  251.8 4.3 convert_reduce_fusion.2
  260.1 3.4 reshape.295
  263.5 16.4 %copy.227 = bf16[6,12,4,2,1024]{1,2,3,0,4:T(4,128)(2,1)} copy(bf16[6,12,4,2,1024]{4,3,1,2,0:T(2,128)(2,1)S(1)} %reshape.295) | data formatting | bytes 2359296 | tf_op jit(solution)/shard_map/reshape | solution.py:169
  279.9 26.2 %reshape.297 = bf16[8,2,36864]{2,1,0:T(2,128)(2,1)S(1)} reshape(bf16[1024,6,2,4,12]{4,3,2,1,0:T(4,128)(2,1)} %bitcast.192) | data formatting | bytes 2359296
  306.1 25.3 %all_to_all.33 = bf16[8,2,36864]{2,1,0:T(2,128)(2,1)} all-to-all(bf16[8,2,36864]{2,1,0:T(2,128)(2,1)S(1)} %reshape.297), channel_id=1, replica_groups=mesh['lon'=16,'lat'=8] {'lat'}, dimensions={0} | all-to-all | bytes 2359296 | tf_op jit(solution)/shard_map/all_to_all | solution.py:172
  331.3 31.1 %reshape.298 = bf16[1024,6,2,4,12]{4,3,2,1,0:T(4,128)(2,1)} reshape(bf16[8,2,36864]{2,1,0:T(2,128)(2,1)} %all_to_all.33) | data formatting | bytes 2359296
  362.5 19.1 %copy.228 = bf16[6,12,4,2,8,128]{5,3,2,1,0,4:T(2,128)(2,1)S(1)} copy(bf16[6,12,4,2,8,128]{1,2,3,0,5,4:T(4,128)(2,1)} %bitcast.193) | data formatting | bytes 2359296 | tf_op jit(solution)/shard_map/all_to_all | solution.py:172
  383.4 3.9 collective-permute-start.5
  387.3 3.6 fusion.80
  390.9 9.4 %copy.232 = bf16[6,12,4,1,1024]{1,2,0,3,4:T(4,128)(2,1)} copy(bf16[6,12,4,1,1024]{4,1,2,0,3:T(8,128)(2,1)} %fusion.80) | data formatting | bytes 1179648 | tf_op jit(solution)/shard_map/reshape | solution.py:165
  400.3 12.3 %reshape.299 = bf16[8,2,18432]{2,1,0:T(2,128)(2,1)} reshape(bf16[1024,1,6,4,12]{4,3,2,1,0:T(4,128)(2,1)} %bitcast.199) | data formatting | bytes 1179648
  412.6 4.2 all-to-all-start.1
  417.3 10.1 %all-to-all-done.1 = bf16[8,2,18432]{2,1,0:T(2,128)(2,1)} async-done(((bf16[8,2,18432]{2,1,0:T(2,128)(2,1)}), bf16[8,2,18432]{2,1,0:T(2,128)(2,1)}, u32[]{:S(2)}, u32[]{:S(2)}) %all-to-all-start.1) | async-done | bytes 589856 | tf_op jit(solution)/shard_map/all_to_all | solution.py:171
  427.4 16.6 %reshape.300 = bf16[1024,1,6,4,12]{4,3,2,1,0:T(4,128)(2,1)} reshape(bf16[8,2,18432]{2,1,0:T(2,128)(2,1)} %all-to-all-done.1) | data formatting | bytes 1179648
  444.0 7.4 copy.259
  454.7 9.7 %select_maximum_fusion = bf16[54,24,4,2,128]{4,3,2,1,0:T(2,128)(2,1)S(1)} fusion(bf16[48,6,4,2,128]{4,3,2,1,0:T(2,128)(2,1)} %collective-permute-done.5, bf16[48,12,4,2,128]{4,3,2,1,0:T(2,128)(2,1)S(1)} %bitcast.203, bf16[48,6,4,2,128]{4,3,2,1,0:T(2,128)(2,1)} %collective-permute-done.4), kind=kLoop, calls=%fused_computation.74 | loop fusion | flops 15925248 | bytes 5013504 | tf_op jit(solution)/shard_map/concatenate | solution.py:18
  466.9 66.5 %while.23 = (s32[]{:T(128)}, bf16[9,2,288,128]{3,2,1,0:T(8,128)(2,1)}, bf16[9,2,288,2,128]{4,2,3,1,0:T(8,128)(2,1)}, f32[9,2,288]{2,1,0:T(2,128)S(1)}, bf16[9,2,...) while((s32[]{:T(128)}, bf16[9,2,288,128]{3,2,1,0:T(8,128)(2,1)}, ...), condition=%wide.region_15.16_spmd.clone, body=%wide.region_12.15_spmd.clone.sunk | while | flops 87248736 | bytes 6705241 | solution.py:84
  536.9 5.8 copy.241
  546.3 197.3 %all-reduce.6.cloned.1.call-done = bf16[48,12,4,1024]{3,2,1,0:T(4,128)(2,1)} async-done(((bf16[48,12,4,1024]{3,2,1,0:T(4,128)(2,1)}), bf16[48,12,4,1024]{3,2,1,0:T(4,128)(2,1)}) %all-reduce.6.cloned.1.call-update) | async-done | bytes 4718608
  (240 shorter events, 145.3 us)
Async XLA Ops:
  7.2 528.4 %copy-start = (bf16[1024,1024]{1,0:T(8,128)(2,1)S(1)}, bf16[1024,1024]{1,0:T(8,128)(2,1)}, u32[]{:S(2)}) copy-start(bf16[1024,1024]{1,0:T(8,128)(2,1)} %param.25) | copy-start | bytes 6291460
  9.2 61.0 %copy-start.3 = (bf16[12,24,4,512]{3,1,2,0:T(8,128)(2,1)}, bf16[12,24,4,512]{3,1,2,0:T(8,128)(2,1)S(1)}, u32[]{:S(2)}) copy-start(bf16[12,24,4,512]{3,1,2,0:T(8,128)(2,1)S(1)} %add_convert_fusion.1) | copy-start | bytes 3538948
  9.4 11.6 %collective-permute-start = (bf16[12,6,4,512]{3,1,2,0:T(8,128)(2,1)S(1)}, bf16[12,6,4,512]{3,1,2,0:T(8,128)(2,1)S(1)}, u32[]{:S(2)}, u32[]{:S(2)}) collective-permute-start(bf16[12,6,4,512]{3,1,2,0:T(8,128)(2,1)S(1)} %get-tuple-element.228), channel_id=1, source_target_pairs={{0,8},{8,16},{16,24},{24,32},{32,40},{40,48},{48,56},{56,64},{64,7... | collective-permute-start | bytes 884744 | tf_op jit(solution)/shard_map/ppermute | solution.py:20
  9.5 11.5 %collective-permute-start.1 = (bf16[12,6,4,512]{3,1,2,0:T(8,128)(2,1)S(1)}, bf16[12,6,4,512]{3,1,2,0:T(8,128)(2,1)S(1)}, u32[]{:S(2)}, u32[]{:S(2)}) collective-permute-start(bf16[12,6,4,512]{3,1,2,0:T(8,128)(2,1)S(1)} %get-tuple-element.229), channel_id=1, source_target_pairs={{8,0},{16,8},{24,16},{32,24},{40,32},{48,40},{56,48},{64,56},{72,6... | collective-permute-start | bytes 884744 | tf_op jit(solution)/shard_map/ppermute | solution.py:22
  20.9 0.8 copy-start.9
  21.7 0.7 copy-start.11
  25.1 26.4 %collective-permute-start.2 = (bf16[6,36,4,512]{3,2,1,0:T(4,128)(2,1)}, bf16[6,36,4,512]{3,2,1,0:T(4,128)(2,1)}, u32[]{:S(2)}, u32[]{:S(2)}) collective-permute-start(bf16[6,36,4,512]{3,2,1,0:T(4,128)(2,1)} %copy.208), channel_id=1, source_target_pairs={{0,1},{1,2},{2,3},{3,4},{4,5},{5,6},{6,7},{7,0},{8,9},{9,10},{10,1... | collective-permute-start | bytes 2654216 | tf_op jit(solution)/shard_map/ppermute | solution.py:20
  29.2 39.7 %collective-permute-start.3 = (bf16[6,36,4,512]{3,2,1,0:T(4,128)(2,1)}, bf16[6,36,4,512]{3,2,1,0:T(4,128)(2,1)}, u32[]{:S(2)}, u32[]{:S(2)}) collective-permute-start(bf16[6,36,4,512]{3,2,1,0:T(4,128)(2,1)} %copy.209), channel_id=1, source_target_pairs={{1,0},{2,1},{3,2},{4,3},{5,4},{6,5},{7,6},{0,7},{9,8},{10,9},{11,1... | collective-permute-start | bytes 2654216 | tf_op jit(solution)/shard_map/ppermute | solution.py:22
  32.8 37.4 %copy-start.10 = (bf16[12,6,4,512]{3,1,2,0:T(8,128)(2,1)S(1)}, bf16[12,6,4,512]{3,1,2,0:T(8,128)(2,1)}, u32[]{:S(2)}) copy-start(bf16[12,6,4,512]{3,1,2,0:T(8,128)(2,1)} %copy-done.9) | copy-start | bytes 884740
  32.8 37.4 %copy-start.12 = (bf16[12,6,4,512]{3,1,2,0:T(8,128)(2,1)S(1)}, bf16[12,6,4,512]{3,1,2,0:T(8,128)(2,1)}, u32[]{:S(2)}) copy-start(bf16[12,6,4,512]{3,1,2,0:T(8,128)(2,1)} %copy-done.11) | copy-start | bytes 884740
  78.2 5.4 copy-start.14
  90.1 13.0 %copy-start.15 = (bf16[512,512]{1,0:T(8,128)(2,1)S(1)}, bf16[512,512]{1,0:T(8,128)(2,1)}, u32[]{:S(2)}) copy-start(bf16[512,512]{1,0:T(8,128)(2,1)} %param.18) | copy-start | bytes 1572868
  124.1 9.5 %copy-start.2 = (bf16[3,288,1,512]{1,3,0,2:T(8,128)(2,1)S(1)}, bf16[3,288,1,512]{1,3,0,2:T(8,128)(2,1)}, u32[]{:S(2)}) copy-start(bf16[3,288,1,512]{1,3,0,2:T(8,128)(2,1)} %get-tuple-element.310) | copy-start | bytes 2654212 | tf_op jit(solution)/shard_map/while
  158.5 9.5 %copy-start.2 = (bf16[3,288,1,512]{1,3,0,2:T(8,128)(2,1)S(1)}, bf16[3,288,1,512]{1,3,0,2:T(8,128)(2,1)}, u32[]{:S(2)}) copy-start(bf16[3,288,1,512]{1,3,0,2:T(8,128)(2,1)} %get-tuple-element.310) | copy-start | bytes 2654212 | tf_op jit(solution)/shard_map/while
  192.9 9.5 %copy-start.2 = (bf16[3,288,1,512]{1,3,0,2:T(8,128)(2,1)S(1)}, bf16[3,288,1,512]{1,3,0,2:T(8,128)(2,1)}, u32[]{:S(2)}) copy-start(bf16[3,288,1,512]{1,3,0,2:T(8,128)(2,1)} %get-tuple-element.310) | copy-start | bytes 2654212 | tf_op jit(solution)/shard_map/while
  219.8 1.3 copy-start.4
  219.8 1.4 copy-start.16
  222.1 1.0 copy-start.13
  232.4 6.8 copy-start.5
  235.3 3.9 copy-start.1
  249.3 7.7 %slice-start = ((s8[6291456]{0:T(1024)(128)(4,1)}), s8[4194304]{0:T(1024)(128)(4,1)S(1)}, s32[]{:S(2)}) async-start(s8[6291456]{0:T(1024)(128)(4,1)} %bitcast.221), calls=%async_computation.3 | async-start | bytes 8388608
  251.8 5.2 slice-start.1
  256.1 0.9 copy-start.7
  381.6 5.7 copy-start.8
  383.4 71.3 %collective-permute-start.4 = (bf16[48,6,4,2,128]{4,3,2,1,0:T(2,128)(2,1)}, bf16[48,6,4,2,128]{4,3,2,1,0:T(2,128)(2,1)}, u32[]{:S(2)}, u32[]{:S(2)}) collective-permute-start(bf16[48,6,4,2,128]{4,3,2,1,0:T(2,128)(2,1)} %get-tuple-element.226), channel_id=1, source_target_pairs={{0,8},{8,16},{16,24},{24,32},{32,40},{40,48},{48,56},{56,64},{64,7... | collective-permute-start | bytes 1769480 | tf_op jit(solution)/shard_map/ppermute | solution.py:20
  383.4 71.3 %collective-permute-start.5 = (bf16[48,6,4,2,128]{4,3,2,1,0:T(2,128)(2,1)}, bf16[48,6,4,2,128]{4,3,2,1,0:T(2,128)(2,1)}, u32[]{:S(2)}, u32[]{:S(2)}) collective-permute-start(bf16[48,6,4,2,128]{4,3,2,1,0:T(2,128)(2,1)} %get-tuple-element.227), channel_id=1, source_target_pairs={{8,0},{16,8},{24,16},{32,24},{40,32},{48,40},{56,48},{64,56},{72,6... | collective-permute-start | bytes 1769480 | tf_op jit(solution)/shard_map/ppermute | solution.py:22
  412.6 14.8 %all-to-all-start.1 = ((bf16[8,2,18432]{2,1,0:T(2,128)(2,1)}), bf16[8,2,18432]{2,1,0:T(2,128)(2,1)}, u32[]{:S(2)}, u32[]{:S(2)}) async-start(bf16[8,2,18432]{2,1,0:T(2,128)(2,1)} %reshape.299), calls=%async_computation.1 | async-start | bytes 1179648 | tf_op jit(solution)/shard_map/all_to_all | solution.py:171
  416.9 326.7 %all-reduce.6.cloned.1.call-start = ((), (), s32[]{:S(2)}) async-start(), calls=%async_computation.2 | async-start | bytes 9437184
  542.7 0.7 copy-start.17
  542.7 1.9 copy-start.6
Sparse Core Ops, SparseCore 0:
  542.9 200.5 all-reduce.5
where the time goes:
time: 763 us; the launch traced here: 755 us
  local copies, waits for them, and re-layouts  296 us (39%)
  waiting for transfers between devices  249 us (33%)
  matrix products  117 us (15%)
  other arithmetic  31.6 us (4%)
  blocking collectives  25.3 us (3%)
  starting transfers between devices  18.9 us (2%)
  between operations  15.5 us (2%)
    unnamed x2, waiting for transfers between devices  197 us
    unnamed x46, local copies, waits for them, and re-layouts  94.9 us
    dynamic_slice x48, local copies, waits for them, and re-layouts, window_attention(): return lax.map(window_row, (query_win, pair_win, valid_win))  56 us
    sub x12, matrix products, window_row(): weights = jnp.exp(scores - row_top)  46.5 us
    dot_general x12, matrix products, window_row(): jnp.einsum('nhqk,nkhd->nqhd', weights_bf, value_heads, preferred_element_...  35 us
    ppermute x3, waiting for transfers between devices, with_halo(): lax.ppermute(tail, axis, [(i, (i + 1) % count) for i in range(count)])  25.5 us
    all_to_all x1, blocking collectives, local(): lax.all_to_all(coarse_pair, 'lat', split_axis=4, concat_axis=0, tiled=True)  25.3 us
    reshape x2, local copies, waits for them, and re-layouts, local(): coarse_pair.reshape(band_rows, band_cols, levels, 2, coarse_width)  19.8 us
  transfers between devices with their start and end apart: 8, of which 5 were waited for; matrix products, arithmetic and copies ran while one was open for 8% of the time, Pallas kernels for 0%

commit v1 on v0

v1 whole, which is shorter than its diff:
```python
import functools
import math

import jax
import jax.numpy as jnp
import numpy as np
from jax import lax
from jax.experimental import pallas as pl
from jax.experimental.pallas import tpu as pltpu
from jax.sharding import PartitionSpec as P

EPS = 1e-05
BR, BC, LEV = 3, 6, 4
ROWS = BR * BC * LEV
PAD = 80
WIN = 4 * ROWS
GRP = WIN // 2
HD = 64
F32 = jnp.float32
BF16 = jnp.bfloat16


def selections():
    out = np.zeros((6, 4 * PAD, 4 * PAD), np.float32)
    for b in range(4):
        for r in range(BR):
            for c in range(BC):
                for l in range(LEV):
                    i = b * PAD + (r * BC + c) * LEV + l
                    slab = (r * 4 * BC + b * BC + c) * LEV + l
                    out[0, i, slab] = 1
                    out[1, slab, i] = 1
                    g = 1 if l in (1, 2) else 0
                    li = (0, 0, 1, 1)[l]
                    win = g * GRP + li * (GRP // 2) + b * BR * BC + r * BC + c
                    out[2, win, i] = 1
                    out[3, i, win] = 1
                    rc = (((b // 2) * BR + r) * 2 * BC + (b % 2) * BC + c) * LEV + l
                    out[5, rc, i] = 1
    for k in range(4):
        for ci in range(BR):
            for cj in range(BC):
                for l in range(LEV):
                    fr, fc = 2 * ci + k % 2, 2 * cj + k // 2
                    b = (fr // BR) * 2 + fc // BC
                    i = b * PAD + ((fr % BR) * BC + fc % BC) * LEV + l
                    out[4, k * PAD + (ci * BC + cj) * LEV + l, i] = 1
    return out


def biases():
    at = np.arange(GRP)
    level = at // (GRP // 2)
    half = at % (GRP // 2) // (GRP // 4)
    same_level = level[:, None] == level[None, :]
    same_half = half[:, None] == half[None, :]
    ok = [same_level, np.ones_like(same_level), same_level & same_half, same_half]
    return np.where(np.stack(ok), 0.0, -1e30).astype(np.float32)


def norm(v):
    v = v.astype(F32)
    c = v - jnp.mean(v, axis=-1, keepdims=True)
    s = jnp.mean(c * c, axis=-1, keepdims=True)
    return (c * lax.rsqrt(s + EPS)).astype(BF16)


def mm(a, b):
    return jnp.dot(a, b, preferred_element_type=F32)


def attention(q, k, v, bias, first_bias, out, width):
    lane = lax.broadcasted_iota(jnp.int32, (GRP, 2 * HD), 1)
    low = lane < HD
    zero = jnp.zeros((GRP, 2 * HD), BF16)
    for g in range(2):
        rows = slice(g * GRP, (g + 1) * GRP)
        b = bias[first_bias + g]
        b = jnp.concatenate([b, b], axis=0)
        for pair in range(width // (2 * HD)):
            lanes = slice(pair * 2 * HD, (pair + 1) * 2 * HD)
            qp = q[rows, lanes]
            qq = jnp.concatenate([jnp.where(low, qp, zero), jnp.where(low, zero, qp)], axis=0)
            s = lax.dot_general(
                qq, k[rows, lanes], (((1,), (1,)), ((), ())), preferred_element_type=F32
            )
            s = s + b
            p = jnp.exp2(s - jnp.max(s, axis=-1, keepdims=True))
            total = jnp.sum(p, axis=-1, keepdims=True)
            o = mm(p.astype(BF16), v[rows, lanes]) / total
            out[rows, lanes] = jnp.where(low, o[:GRP], o[GRP:]).astype(BF16)


def kernel(
    n_lat, n_lon, x, code, table, sel_h, bias_h,
    wq_h, wkv_h, wo_h, w1_h, w2_h, wm_h, wc_h, wco_h,
    fine, coarse,
    sel, bias, wq, wkv, wo, w1, w2, wm, wc, wco,
    emb, fs, rt, rl, rd, q, k, v, att, aft,
    merged, cin, cq, ck, cv, catt, cs, cr,
    load_sem, s1, r1, s2, r2, s3, r3, s4, r4,
):
    lat, lon = lax.axis_index("lat"), lax.axis_index("lon")
    up, down = lax.rem(lat + n_lat - 1, n_lat), lax.rem(lat + 1, n_lat)
    left, right = lax.rem(lon + n_lon - 1, n_lon), lax.rem(lon + 1, n_lon)

    loads = {}
    for at, (name, src, dst) in enumerate([
        ("sel", sel_h, sel), ("wq", wq_h, wq), ("wkv", wkv_h, wkv), ("bias", bias_h, bias),
        ("wo", wo_h, wo), ("w1", w1_h, w1), ("w2", w2_h, w2), ("wm", wm_h, wm),
        ("wc", wc_h, wc), ("wco", wco_h, wco),
    ]):
        loads[name] = pltpu.make_async_copy(src, dst, load_sem.at[at])
        loads[name].start()

    places = [(up, lon), (lat, left), (up, left), (down, lon), (lat, right), (down, right)]
    barrier = pltpu.get_barrier_semaphore()
    for a, o in places:
        pl.semaphore_signal(
            barrier, inc=1, device_id={"lat": a, "lon": o}, device_id_type=pl.DeviceIdType.MESH
        )

    def send(src, dst, ssem, rsem, a, o):
        return pltpu.make_async_remote_copy(
            src_ref=src, dst_ref=dst, send_sem=ssem, recv_sem=rsem,
            device_id={"lat": a, "lon": o}, device_id_type=pl.DeviceIdType.MESH,
        )

    def shift_up(grid, ssem, rsem):
        return [
            send(grid.at[0, 0], grid.at[4, 4], ssem.at[0], rsem.at[0], up, left),
            send(grid.at[0, 1], grid.at[4, 1], ssem.at[1], rsem.at[1], up, lon),
            send(grid.at[0, pl.ds(2, 2)], grid.at[4, pl.ds(2, 2)], ssem.at[2], rsem.at[2], up, lon),
            send(grid.at[1, 0], grid.at[1, 4], ssem.at[3], rsem.at[3], lat, left),
            send(grid.at[pl.ds(2, 2), 0], grid.at[pl.ds(2, 2), 4], ssem.at[4], rsem.at[4], lat, left),
        ]

    loads["sel"].wait()
    ids = lax.broadcasted_iota(jnp.int32, (16, WIN), 0)
    for s in range(4):
        hot = (ids == code[s]).astype(F32).astype(BF16)
        kind = lax.dot_general(
            hot, table[...], (((0,), (0,)), ((), ())), preferred_element_type=F32
        )
        e = (x[s * WIN:(s + 1) * WIN].astype(F32) + kind).astype(BF16)
        e = mm(sel[0][:, :WIN], e).astype(BF16)
        for b in range(4):
            emb[s, b] = e[b * PAD:(b + 1) * PAD]

    pl.semaphore_wait(barrier, len(places))
    first = shift_up(emb, s1, r1)
    for at in (3, 4, 1, 2, 0):
        first[at].start()

    for name in ("wq", "wkv", "bias", "wo", "w1", "w2"):
        loads[name].wait()
    second = shift_up(fs, s2, r2)
    back = [
        send(fs.at[pl.ds(0, 2), 3], rl.at[pl.ds(0, 2)], s3.at[0], r3.at[0], lat, right),
        send(fs.at[2, 3], rl.at[2], s3.at[1], r3.at[1], lat, right),
        send(fs.at[3, pl.ds(0, 2)], rt.at[pl.ds(0, 2)], s3.at[2], r3.at[2], down, lon),
        send(fs.at[3, 2], rt.at[2], s3.at[3], r3.at[3], down, lon),
        send(fs.at[3, 3], rd, s3.at[4], r3.at[4], down, right),
    ]
    scale = math.log2(math.e) / math.sqrt(HD)

    def window(w, carry):
        wr, wc_ = w // 2, w % 2

        @pl.when(w == 1)
        def _():
            first[3].wait_recv()
            first[4].wait_recv()

        @pl.when(w == 2)
        def _():
            first[1].wait_recv()
            first[2].wait_recv()

        @pl.when(w == 3)
        def _():
            first[0].wait_recv()

        r0, c0 = 1 + 2 * wr, 1 + 2 * wc_
        blocks = [emb[r0, c0], emb[r0, c0 + 1], emb[r0 + 1, c0], emb[r0 + 1, c0 + 1]]
        e = mm(sel[2][:WIN], jnp.concatenate(blocks, axis=0))
        aft[...] = e.astype(BF16)
        n = norm(e)
        q[...] = (mm(n, wq[...]) * scale).astype(BF16)
        k[...] = mm(n, wkv[:, :512]).astype(BF16)
        v[...] = mm(n, wkv[:, 512:]).astype(BF16)
        wrapped = jnp.where((lat == n_lat - 1) & (wr == 1), 2, 0)
        attention(q, k, v, bias, wrapped, att, 512)
        a = (aft[...].astype(F32) + mm(att[...], wo[...])).astype(BF16)
        aft[...] = a
        n = norm(a)
        acc = a.astype(F32)
        for j in range(0, 2048, 512):
            h = jax.nn.gelu(mm(n, w1[:, j:j + 512])).astype(BF16)
            acc = acc + mm(h, w2[j:j + 512])
        f = mm(sel[3][:, :WIN], acc.astype(BF16)).astype(BF16)
        r0, c0 = 2 * wr, 2 * wc_
        for b in range(4):
            fs[r0 + b // 2, c0 + b % 2] = f[b * PAD:(b + 1) * PAD]

        @pl.when(w == 0)
        def _():
            second[0].start()
            second[1].start()
            second[3].start()

        @pl.when(w == 1)
        def _():
            second[2].start()
            back[0].start()

        @pl.when(w == 2)
        def _():
            second[4].start()
            back[2].start()

        @pl.when(w == 3)
        def _():
            back[1].start()
            back[3].start()
            back[4].start()

        return carry

    lax.fori_loop(0, 4, window, 0)

    def quadrant(w, carry):
        wr, wc_ = w // 2, w % 2

        @pl.when(w == 1)
        def _():
            second[3].wait_recv()
            second[4].wait_recv()

        @pl.when(w == 2)
        def _():
            second[1].wait_recv()
            second[2].wait_recv()

        @pl.when(w == 3)
        def _():
            second[0].wait_recv()

        r0, c0 = 1 + 2 * wr, 1 + 2 * wc_
        blocks = [fs[r0, c0], fs[r0, c0 + 1], fs[r0 + 1, c0], fs[r0 + 1, c0 + 1]]
        m = mm(sel[4], jnp.concatenate(blocks, axis=0))
        m = jnp.concatenate([m[j * PAD:(j + 1) * PAD] for j in range(4)], axis=1)
        merged[w] = norm(m)
        return carry

    lax.fori_loop(0, 4, quadrant, 0)

    loads["wm"].wait()
    m = jnp.concatenate([merged[j] for j in range(4)], axis=0)
    for j in range(0, 1024, 512):
        t = mm(m, wm[:, j:j + 512]).astype(BF16)
        cin[:, j:j + 512] = mm(sel[2][:WIN], t).astype(BF16)
    n = norm(cin[...])
    loads["wc"].wait()
    for j in range(0, 1024, 512):
        cq[:, j:j + 512] = (mm(n, wc[:, j:j + 512]) * scale).astype(BF16)
        ck[:, j:j + 512] = mm(n, wc[:, 1024 + j:1536 + j]).astype(BF16)
        cv[:, j:j + 512] = mm(n, wc[:, 2048 + j:2560 + j]).astype(BF16)
    attention(cq, ck, cv, bias, jnp.where(lat == n_lat - 1, 2, 0), catt, 1024)
    loads["wco"].wait()
    for j in range(0, 1024, 512):
        t = (cin[:, j:j + 512].astype(F32) + mm(catt[...], wco[:, j:j + 512])).astype(BF16)
        t = mm(sel[3][:, :WIN], t).astype(BF16)
        for b in range(4):
            cs[b, :, j:j + 512] = t[b * PAD:(b + 1) * PAD]
    third = [
        send(cs.at[1], cr.at[1], s4.at[0], r4.at[0], lat, right),
        send(cs.at[2], cr.at[2], s4.at[1], r4.at[1], down, lon),
        send(cs.at[3], cr.at[0], s4.at[2], r4.at[2], down, right),
    ]
    for copy in third:
        copy.start()

    for copy in back:
        copy.wait_recv()
    for s in range(4):
        if s == 0:
            blocks = [rd[...], rt[0], rt[1], rt[2]]
        else:
            blocks = [rl[s - 1], fs[s - 1, 0], fs[s - 1, 1], fs[s - 1, 2]]
        fine[s * WIN:(s + 1) * WIN] = mm(sel[1][:WIN], jnp.concatenate(blocks, axis=0)).astype(BF16)

    for copy in third:
        copy.wait_recv()
    blocks = [cr[0], cr[2], cr[1], cs[0]]
    coarse[...] = mm(sel[5][:WIN], jnp.concatenate(blocks, axis=0)).astype(BF16)
    for copy in first + second + back + third:
        copy.wait_send()


def local(
    n_lat, n_lon, tokens, surface_kind, kind_table, attn_q_w, attn_kv_w, attn_out_w,
    mlp_in_w, mlp_out_w, merge_w, coarse_qkv_w, coarse_out_w,
):
    rows, cols, lev, width = tokens.shape
    x = tokens.reshape(rows * cols * lev, width)
    code = surface_kind[:, :, None] * lev + jnp.arange(lev, dtype=jnp.int32)
    code = code.reshape(4, 1, WIN)
    table = jnp.pad(kind_table.reshape(-1, width), ((0, 4), (0, 0)))
    sel = jnp.asarray(selections(), BF16)
    bias = jnp.asarray(biases())
    weights = [attn_q_w, attn_kv_w, attn_out_w, mlp_in_w, mlp_out_w, merge_w, coarse_qkv_w, coarse_out_w]
    vmem, hbm = pl.BlockSpec(memory_space=pltpu.VMEM), pl.BlockSpec(memory_space=pl.ANY)
    dma = pltpu.SemaphoreType.DMA
    buf = lambda *shape: pltpu.VMEM(shape, BF16)
    fine, coarse = pl.pallas_call(
        functools.partial(kernel, n_lat, n_lon),
        out_shape=(
            jax.ShapeDtypeStruct((4 * WIN, width), BF16),
            jax.ShapeDtypeStruct((WIN, 2 * width), BF16),
        ),
        in_specs=[vmem] * 3 + [hbm] * 10,
        out_specs=(vmem, vmem),
        scratch_shapes=[
            buf(*sel.shape), pltpu.VMEM(bias.shape, F32), *[buf(*w.shape) for w in weights],
            buf(5, 5, PAD, width), buf(5, 5, PAD, width),
            buf(3, PAD, width), buf(3, PAD, width), buf(PAD, width),
            *[buf(WIN, width)] * 5,
            buf(4, PAD, 4 * width), *[buf(WIN, 2 * width)] * 5,
            buf(4, PAD, 2 * width), buf(3, PAD, 2 * width),
            dma((10,)), dma((5,)), dma((5,)), dma((5,)), dma((5,)), dma((5,)), dma((5,)),
            dma((3,)), dma((3,)),
        ],
        compiler_params=pltpu.CompilerParams(
            collective_id=0, has_side_effects=True, vmem_limit_bytes=60 * 1024 * 1024
        ),
        name="block",
    )(x, code, table, sel, bias, *weights)
    return (
        fine.reshape(rows, cols, lev, width),
        coarse.reshape(rows // 2, cols // 2, lev, 2 * width),
    )


def solution(mesh):
    grid = P("lat", "lon", None, None)
    return jax.shard_map(
        functools.partial(local, mesh.shape["lat"], mesh.shape["lon"]),
        mesh=mesh,
        in_specs=(grid, P("lat", "lon")) + (P(),) * 9,
        out_specs=(grid, grid),
        check_vma=False,
    )
```

time: 763 us -> 64.9 us (0.09)
  the two profiles are of different devices: /device:TPU:0 before, /device:TPU:1 now
where the time goes in v1:
time: 64.9 us; the launch traced here: 64.6 us
  Pallas kernels  53.5 us (82%)
  local copies, waits for them, and re-layouts  9.59 us (15%)
  other arithmetic  0.8 us (1%)
  between operations  0.66 us (1%)
    pallas_call x1, Pallas kernels, local(): pl.pallas_call(functools.partial(kernel, n_lat, n_lon), out_shape=(jax.Sh...  53.5 us
    reshape x1, local copies, waits for them, and re-layouts, local(): fine.reshape(rows, cols, lev, width)  3.33 us
    reshape x1, local copies, waits for them, and re-layouts, local(): x = tokens.reshape(rows * cols * lev, width)  3.16 us

profile of v1, /device:TPU:1, one launch (start us, length us, event | category | flops | bytes accessed | tf_op | source)
XLA Modules:
  0.0 64.6 jit_solution(17463919943930196923)
XLA Ops:
  0.6 0.7 %broadcast_multiply_fusion = s32[12,24]{1,0:T(8,128)S(1)} fusion(s32[12,24]{1,0:T(8,128)} %param.14), kind=kLoop, calls=%fused_computation.1 | loop fusion | flops 288 | bytes 2304 | tf_op jit(solution)/shard_map/mul | solution.py:307
  1.3 0.7 %reshape.38 = bf16[12,512]{1,0:T(8,128)(2,1)S(1)} reshape(bf16[3,4,512]{2,1,0:T(4,128)(2,1)} %param.15) | data formatting | bytes 24576 | tf_op jit(solution)/shard_map/reshape | solution.py:309
  2.0 0.6 pad.4.table
  2.7 0.1 iota_add_fusion
  2.8 0.7 %add.29.code = s32[4,1,288]{2,1,0:T(1,128)} reshape(s32[12,24,4]{2,1,0:T(8,128)S(1)} %iota_add_fusion) | data formatting | bytes 9216 | tf_op jit(solution)/shard_map/add | solution.py:307
  3.5 3.2 %reshape.37.x = bf16[1152,512]{1,0:T(8,128)(2,1)} reshape(bf16[12,24,4,512]{3,2,1,0:T(4,128)(2,1)} %param.13) | data formatting | bytes 2359296 | tf_op jit(solution)/shard_map/reshape | solution.py:306
  6.7 53.5 %block.1 = (bf16[1152,512]{1,0:T(8,128)(2,1)}, bf16[288,1024]{1,0:T(8,128)(2,1)}) custom-call(bf16[1152,512]{1,0:T(8,128)(2,1)} %reshape.37.x, s32[4,1,288]{2,1,0:T(1,128)} %add.29.code, bf16[16,512]{1,0:T(8,128)(2,1)} %pad.4.table, bf16[6,320,320]{2,1,0:T(8,128)(2,1)} %constant.9.clone.sel_h, f32[4,144,144]{2,1,0:T(8,128)} %constant.10.clone.bias_h, ...), custom_call_target="tpu_custom_call" | custom-call | tf_op jit(solution)/shard_map/block/pallas_call | solution.py:316
  60.2 0.0 copy-start
  60.2 3.3 %reshape.39 = bf16[12,24,4,512]{3,2,1,0:T(4,128)(2,1)} reshape(bf16[1152,512]{1,0:T(8,128)(2,1)} %get-tuple-element.4) | data formatting | bytes 2359296 | tf_op jit(solution)/shard_map/reshape | solution.py:340
  63.5 0.0 copy-done
  63.5 1.0 %reshape.40 = bf16[6,12,4,1024]{3,2,1,0:T(4,128)(2,1)} reshape(bf16[288,1024]{1,0:T(8,128)(2,1)S(1)} %copy-done) | data formatting | bytes 1179648 | tf_op jit(solution)/shard_map/reshape | solution.py:341
Async XLA Ops:
  60.2 3.3 %copy-start = (bf16[288,1024]{1,0:T(8,128)(2,1)S(1)}, bf16[288,1024]{1,0:T(8,128)(2,1)}, u32[]{:S(2)}) copy-start(bf16[288,1024]{1,0:T(8,128)(2,1)} %get-tuple-element.5) | copy-start | bytes 1769476

commit v2 on v1

v2 whole, which is shorter than its diff:
```python
import functools
import math

import jax
import jax.numpy as jnp
import numpy as np
from jax import lax
from jax.experimental import pallas as pl
from jax.experimental.pallas import tpu as pltpu
from jax.sharding import PartitionSpec as P

EPS = 1e-05
LEV = 4
WR, WC = 6, 12
SR, SC = WR // 2, WC // 2
WIN = WR * WC * LEV
GRP = WIN // 2
HD = 64
F32 = jnp.float32
BF16 = jnp.bfloat16


def orders():
    out = np.zeros((2, WIN, WIN), np.float32)
    for r in range(WR):
        for c in range(WC):
            for l in range(LEV):
                nat = (r * WC + c) * LEV + l
                g = 1 if l in (1, 2) else 0
                win = g * GRP + (l // 2) * (GRP // 2) + r * WC + c
                out[0, win, nat] = 1
                out[1, nat, win] = 1
    return out


def biases():
    at = np.arange(GRP)
    level = at // (GRP // 2)
    half = at % (GRP // 2) // (GRP // 4)
    same_level = level[:, None] == level[None, :]
    same_half = half[:, None] == half[None, :]
    ok = [same_level, np.ones_like(same_level), same_level & same_half, same_half]
    return np.where(np.stack(ok), 0.0, -1e30).astype(np.float32)


def norm(v):
    v = v.astype(F32)
    c = v - jnp.mean(v, axis=-1, keepdims=True)
    s = jnp.mean(c * c, axis=-1, keepdims=True)
    return (c * lax.rsqrt(s + EPS)).astype(BF16)


def mm(a, b):
    return jnp.dot(a, b, preferred_element_type=F32)


def attention(q, k, v, bias, first_bias, out, width):
    lane = lax.broadcasted_iota(jnp.int32, (GRP, 2 * HD), 1)
    low = lane < HD
    zero = jnp.zeros((GRP, 2 * HD), BF16)
    for g in range(2):
        rows = slice(g * GRP, (g + 1) * GRP)
        b = bias[first_bias + g]
        b = jnp.concatenate([b, b], axis=0)
        for pair in range(width // (2 * HD)):
            lanes = slice(pair * 2 * HD, (pair + 1) * 2 * HD)
            qp = q[rows, lanes]
            qq = jnp.concatenate([jnp.where(low, qp, zero), jnp.where(low, zero, qp)], axis=0)
            s = lax.dot_general(
                qq, k[rows, lanes], (((1,), (1,)), ((), ())), preferred_element_type=F32
            )
            s = s + b
            p = jnp.exp2(s - jnp.max(s, axis=-1, keepdims=True))
            total = jnp.sum(p, axis=-1, keepdims=True)
            o = mm(p.astype(BF16), v[rows, lanes]) / total
            out[rows, lanes] = jnp.where(low, o[:GRP], o[GRP:]).astype(BF16)


def kernel(
    n_lat, n_lon, x, kind, table, sel_h, bias_h,
    wq_h, wkv_h, wo_h, w1_h, w2_h, wm_h, wc_h, wco_h,
    fine, coarse,
    sel, bias, wq, wkv, wo, w1, w2, wm, wc, wco,
    emb, fs, q, k, v, att, aft, hid, cin, cq, ck, cv, catt, cs,
    load_sem, own_sem, s1, r1, s2, r2, s3, r3, s4, r4,
):
    lat, lon = lax.axis_index("lat"), lax.axis_index("lon")
    up, down = lax.rem(lat + n_lat - 1, n_lat), lax.rem(lat + 1, n_lat)
    left, right = lax.rem(lon + n_lon - 1, n_lon), lax.rem(lon + 1, n_lon)
    rows, cols = x.shape[0], x.shape[1]

    loads = {}
    for at, (name, src, dst) in enumerate([
        ("x", x, emb.at[pl.ds(0, rows), pl.ds(0, cols)]),
        ("sel", sel_h, sel), ("wq", wq_h, wq), ("wkv", wkv_h, wkv), ("bias", bias_h, bias),
        ("wo", wo_h, wo), ("w1", w1_h, w1), ("w2", w2_h, w2), ("wm", wm_h, wm),
        ("wc", wc_h, wc), ("wco", wco_h, wco),
    ]):
        loads[name] = pltpu.make_async_copy(src, dst, load_sem.at[at])
        loads[name].start()

    places = [(up, lon), (lat, left), (up, left), (down, lon), (lat, right), (down, right)]
    barrier = pltpu.get_barrier_semaphore()
    for a, o in places:
        pl.semaphore_signal(
            barrier, inc=1, device_id={"lat": a, "lon": o}, device_id_type=pl.DeviceIdType.MESH
        )

    def send(src, dst, ssem, rsem, a, o):
        return pltpu.make_async_remote_copy(
            src_ref=src, dst_ref=dst, send_sem=ssem, recv_sem=rsem,
            device_id={"lat": a, "lon": o}, device_id_type=pl.DeviceIdType.MESH,
        )

    def part(ref, r, c):
        return ref.at[pl.ds(r[0], r[1] - r[0]), pl.ds(c[0], c[1] - c[0])]

    def shift_up(grid, pieces, ssem, rsem):
        out = []
        for at, (r, c) in enumerate(pieces):
            a, o, rr, cc = lat, lon, r, c
            if r[1] <= SR:
                a, rr = up, (r[0] + rows, r[1] + rows)
            if c[1] <= SC:
                o, cc = left, (c[0] + cols, c[1] + cols)
            out.append(send(part(grid, r, c), part(grid, rr, cc), ssem.at[at], rsem.at[at], a, o))
        return out

    def shift_down(grid, place, pieces, n_rows, n_cols, ssem, rsem):
        out = []
        for at, (r, c) in enumerate(pieces):
            a, o = lat, lon
            rr, cc = (r[0] + SR, r[1] + SR), (c[0] + SC, c[1] + SC)
            if rr[0] >= n_rows:
                a, rr = down, (rr[0] - n_rows, rr[1] - n_rows)
            if cc[0] >= n_cols:
                o, cc = right, (cc[0] - n_cols, cc[1] - n_cols)
            out.append(send(part(grid, r, c), part(place, rr, cc), ssem.at[at], rsem.at[at], a, o))
        return out

    loads["x"].wait()
    kinds = kind[...].astype(F32)
    table_rows = jnp.concatenate([table[...], jnp.zeros_like(table[:1])], axis=0).reshape(16, -1)
    band = (SR, cols * LEV, cols)
    here = lax.broadcasted_iota(jnp.int32, band, 1) // LEV == lax.broadcasted_iota(jnp.int32, band, 2)
    n_tok = SR * cols * LEV
    lane = lax.broadcasted_iota(jnp.int32, (n_tok, 16), 1)
    level = lax.broadcasted_iota(jnp.int32, (n_tok, 16), 0) % LEV
    lane_level = (lane % LEV == level)
    lane_kind = (lane // LEV).astype(F32)
    for s in range(0, rows, SR):
        spread = jnp.broadcast_to(kinds[s:s + SR][:, None, :], band)
        own = jnp.sum(jnp.where(here, spread, 0.0), axis=-1, keepdims=True).reshape(n_tok, 1)
        hot = jnp.where(lane_level & (lane_kind == own), 1.0, 0.0).astype(BF16)
        e = emb[s:s + SR, :cols].reshape(n_tok, -1).astype(F32) + mm(hot, table_rows)
        emb[s:s + SR, :cols] = e.astype(BF16).reshape(SR, cols, LEV, -1)

    pl.semaphore_wait(barrier, len(places))
    first = shift_up(
        emb, [((3, 9), (0, 6)), ((0, 3), (6, 18)), ((0, 3), (0, 6)), ((0, 3), (18, 24)), ((9, 12), (0, 6))],
        s1, r1,
    )
    for copy in first:
        copy.start()
    second = shift_up(
        fs, [((0, 3), (0, 6)), ((0, 3), (6, 12)), ((3, 6), (0, 6)), ((0, 3), (12, 24)), ((6, 12), (0, 6))],
        s2, r2,
    )
    back = shift_down(
        fs, fine,
        [((0, 6), (18, 24)), ((9, 12), (0, 12)), ((6, 9), (18, 24)), ((9, 12), (12, 18)), ((9, 12), (18, 24))],
        rows, cols, s3, r3,
    )
    keep = pltpu.make_async_copy(
        part(fs, (0, rows - SR), (0, cols - SC)), part(fine, (SR, rows), (SC, cols)), own_sem.at[0]
    )
    scale = math.log2(math.e) / math.sqrt(HD)
    loads["sel"].wait()

    def window(w, carry):
        wr, wc_ = w // 2, w % 2

        @pl.when(w == 0)
        def _():
            for name in ("wq", "wkv", "bias"):
                loads[name].wait()

        @pl.when(w == 1)
        def _():
            first[0].wait_recv()

        @pl.when(w == 2)
        def _():
            first[1].wait_recv()

        @pl.when(w == 3)
        def _():
            for copy in first[2:]:
                copy.wait_recv()

        e = emb[pl.ds(SR + WR * wr, WR), pl.ds(SC + WC * wc_, WC)].reshape(WIN, -1)
        aft[...] = e
        n = mm(sel[0], norm(e)).astype(BF16)
        q[...] = (mm(n, wq[...]) * scale).astype(BF16)
        k[...] = mm(n, wkv[:, :512]).astype(BF16)
        v[...] = mm(n, wkv[:, 512:]).astype(BF16)
        wrapped = jnp.where((lat == n_lat - 1) & (wr == 1), 2, 0)
        attention(q, k, v, bias, wrapped, att, 512)

        @pl.when(w == 0)
        def _():
            for name in ("wo", "w1", "w2"):
                loads[name].wait()

        mixed = mm(sel[1], att[...]).astype(BF16)
        a = (aft[...].astype(F32) + mm(mixed, wo[...])).astype(BF16)
        aft[...] = a
        n = norm(a)
        for j in range(0, 2048, 512):
            hid[:, j:j + 512] = jax.nn.gelu(mm(n, w1[:, j:j + 512])).astype(BF16)
        f = (aft[...].astype(F32) + mm(hid[...], w2[...])).astype(BF16)
        fs[pl.ds(WR * wr, WR), pl.ds(WC * wc_, WC)] = f.reshape(WR, WC, LEV, -1)

        @pl.when(w == 0)
        def _():
            for copy in second[:3]:
                copy.start()

        @pl.when(w == 1)
        def _():
            second[3].start()
            back[0].start()

        @pl.when(w == 2)
        def _():
            second[4].start()
            back[1].start()

        @pl.when(w == 3)
        def _():
            for copy in back[2:]:
                copy.start()
            keep.start()

        return carry

    lax.fori_loop(0, 4, window, 0)

    loads["wm"].wait()
    for copy in second:
        copy.wait_recv()
    f = fs[pl.ds(SR, rows), pl.ds(SC, cols)].reshape(rows // 2, 2, cols // 2, 2, LEV, -1)
    m = norm(jnp.concatenate([f[:, j % 2, :, j // 2].reshape(WIN, -1) for j in range(4)], axis=1))
    for j in range(0, 1024, 512):
        cin[:, j:j + 512] = mm(m, wm[:, j:j + 512]).astype(BF16)
    n = mm(sel[0], norm(cin[...])).astype(BF16)
    loads["wc"].wait()
    for j in range(0, 1024, 512):
        cq[:, j:j + 512] = (mm(n, wc[:, j:j + 512]) * scale).astype(BF16)
        ck[:, j:j + 512] = mm(n, wc[:, 1024 + j:1536 + j]).astype(BF16)
        cv[:, j:j + 512] = mm(n, wc[:, 2048 + j:2560 + j]).astype(BF16)
    attention(cq, ck, cv, bias, jnp.where(lat == n_lat - 1, 2, 0), catt, 1024)
    loads["wco"].wait()
    mixed = mm(sel[1], catt[...]).astype(BF16)
    for j in range(0, 1024, 512):
        t = (cin[:, j:j + 512].astype(F32) + mm(mixed, wco[:, j:j + 512])).astype(BF16)
        cs[:, :, :, j:j + 512] = t.reshape(WR, WC, LEV, -1)
    third = shift_down(
        cs, coarse, [((0, 3), (6, 12)), ((3, 6), (0, 6)), ((3, 6), (6, 12))], WR, WC, s4, r4
    )
    for copy in third:
        copy.start()
    keep_too = pltpu.make_async_copy(
        part(cs, (0, SR), (0, SC)), part(coarse, (SR, WR), (SC, WC)), own_sem.at[1]
    )
    keep_too.start()
    for copy in back + third:
        copy.wait_recv()
    keep.wait()
    keep_too.wait()
    for copy in first + second + back + third:
        copy.wait_send()


def local(
    n_lat, n_lon, tokens, surface_kind, kind_table, attn_q_w, attn_kv_w, attn_out_w,
    mlp_in_w, mlp_out_w, merge_w, coarse_qkv_w, coarse_out_w,
):
    rows, cols, lev, width = tokens.shape
    sel = jnp.asarray(orders(), BF16)
    bias = jnp.asarray(biases())
    weights = [attn_q_w, attn_kv_w, attn_out_w, mlp_in_w, mlp_out_w, merge_w, coarse_qkv_w, coarse_out_w]
    vmem, hbm = pl.BlockSpec(memory_space=pltpu.VMEM), pl.BlockSpec(memory_space=pl.ANY)
    dma = pltpu.SemaphoreType.DMA
    buf = lambda *shape: pltpu.VMEM(shape, BF16)
    frame = buf(rows + SR, cols + SC, lev, width)
    return pl.pallas_call(
        functools.partial(kernel, n_lat, n_lon),
        out_shape=(
            jax.ShapeDtypeStruct((rows, cols, lev, width), BF16),
            jax.ShapeDtypeStruct((rows // 2, cols // 2, lev, 2 * width), BF16),
        ),
        in_specs=[hbm, vmem, vmem] + [hbm] * 10,
        out_specs=(hbm, hbm),
        scratch_shapes=[
            buf(*sel.shape), pltpu.VMEM(bias.shape, F32), *[buf(*w.shape) for w in weights],
            frame, frame, *[buf(WIN, width)] * 5, buf(WIN, 4 * width), *[buf(WIN, 2 * width)] * 5,
            buf(WR, WC, lev, 2 * width),
            dma((11,)), dma((2,)), dma((5,)), dma((5,)), dma((5,)), dma((5,)), dma((5,)), dma((5,)),
            dma((3,)), dma((3,)),
        ],
        compiler_params=pltpu.CompilerParams(
            collective_id=0, has_side_effects=True, vmem_limit_bytes=60 * 1024 * 1024
        ),
        name="block",
    )(tokens, surface_kind, kind_table, sel, bias, *weights)


def solution(mesh):
    grid = P("lat", "lon", None, None)
    return jax.shard_map(
        functools.partial(local, mesh.shape["lat"], mesh.shape["lon"]),
        mesh=mesh,
        in_specs=(grid, P("lat", "lon")) + (P(),) * 9,
        out_specs=(grid, grid),
        check_vma=False,
    )
```

time: 64.9 us -> 50.1 us (0.77)
  Pallas kernels: 53.5 us -> 45.6 us
  local copies, waits for them, and re-layouts: 9.59 us -> 3.66 us
  other arithmetic: 0.8 us -> 0 us
    reshape x4 -> x0, local copies, waits for them, and re-layouts: 8.24 us -> none  [the longest x1 3.33 us: local(): fine.reshape(rows, cols, lev, width)]
    pallas_call x1, Pallas kernels: 53.5 us -> 45.6 us  [local(): pl.pallas_call(functools.partial(kernel, n_lat, n_lon), out_shape=(jax.Sh...]
    unnamed x2 -> x4, local copies, waits for them, and re-layouts: 0.01 us -> 3.66 us
    add x1 -> x0, local copies, waits for them, and re-layouts: 0.73 us -> none  [local(): code = surface_kind[:, :, None] * lev + jnp.arange(lev, dtype=jnp.int32)]
    mul x1 -> x0, other arithmetic: 0.7 us -> none  [local(): code = surface_kind[:, :, None] * lev + jnp.arange(lev, dtype=jnp.int32)]
where the time goes in v2:
time: 50.1 us; the launch traced here: 49.9 us
  Pallas kernels  45.6 us (91%)
  local copies, waits for them, and re-layouts  3.66 us (7%)
  between operations  0.65 us (1%)
    pallas_call x1, Pallas kernels, local(): pl.pallas_call(functools.partial(kernel, n_lat, n_lon), out_shape=(jax.Sh...  45.6 us
    unnamed x4, local copies, waits for them, and re-layouts  3.66 us

profile of v2, /device:TPU:1, one launch (start us, length us, event | category | flops | bytes accessed | tf_op | source)
XLA Modules:
  0.0 49.9 jit_solution(443824401371439448)
XLA Ops:
  0.6 45.6 %block.1 = (bf16[12,24,4,512]{3,2,1,0:T(4,128)(2,1)}, bf16[6,12,4,1024]{3,2,1,0:T(4,128)(2,1)}) custom-call(bf16[12,24,4,512]{3,2,1,0:T(4,128)(2,1)} %x.1, s32[12,24]{1,0:T(8,128)} %kind.1, bf16[3,4,512]{2,1,0:T(4,128)(2,1)} %table.1, bf16[2,288,288]{2,1,0:T(8,128)(2,1)} %constant.4.clone.sel_h, f32[4,144,144]{2,1,0:T(8,128)} %constant.5.clone.bias_h, ...), custom_call_target="tpu_custom_call" | custom-call | tf_op jit(solution)/shard_map/block/pallas_call | solution.py:297
  46.2 0.0 copy-start
  46.2 2.8 %copy.17 = bf16[12,24,4,512]{3,2,1,0:T(4,128)(2,1)} copy(bf16[12,24,4,512]{3,2,1,0:T(4,128)(2,1)} %get-tuple-element.4) | data formatting | bytes 2359296
  49.1 0.0 copy-done
  49.1 0.8 %copy.18 = bf16[6,12,4,1024]{3,2,1,0:T(4,128)(2,1)} copy(bf16[6,12,4,1024]{3,2,1,0:T(4,128)(2,1)S(1)} %copy-done) | data formatting | bytes 1179648
Async XLA Ops:
  46.2 2.9 %copy-start = (bf16[6,12,4,1024]{3,2,1,0:T(4,128)(2,1)S(1)}, bf16[6,12,4,1024]{3,2,1,0:T(4,128)(2,1)}, u32[]{:S(2)}) copy-start(bf16[6,12,4,1024]{3,2,1,0:T(4,128)(2,1)} %get-tuple-element.5) | copy-start | bytes 1769476

commit v3 on v2

v3 whole, which is shorter than its diff:
```python
import functools
import math

import jax
import jax.numpy as jnp
import numpy as np
from jax import lax
from jax.experimental import pallas as pl
from jax.experimental.pallas import tpu as pltpu
from jax.sharding import PartitionSpec as P

EPS = 1e-05
LEV = 4
WR, WC = 6, 12
SR, SC = WR // 2, WC // 2
WIN = WR * WC * LEV
GRP = WIN // 2
POS = WR * WC
QPAD = 40
GROUPS = ((0, 3), (1, 2))
HD = 64
LANES = 128
F32 = jnp.float32
BF16 = jnp.bfloat16


def biases():
    at = np.arange(GRP)
    level = at // POS
    half = at % POS // (POS // 2)
    same_level = level[:, None] == level[None, :]
    same_half = half[:, None] == half[None, :]
    ok = [same_level, np.ones_like(same_level), same_level & same_half, same_half]
    full = np.where(np.stack(ok), 0.0, -1e30).astype(np.float32)
    halves = np.zeros((4, 2, 2, QPAD, GRP), np.float32)
    halves[:, :, :, :POS // 2] = full.reshape(4, 2, 2, POS // 2, GRP).transpose(0, 2, 1, 3, 4)
    return full, halves.reshape(8, 2 * QPAD, GRP)


def norm(v):
    v = v.astype(F32)
    c = v - jnp.mean(v, axis=-1, keepdims=True)
    s = jnp.mean(c * c, axis=-1, keepdims=True)
    return c * lax.rsqrt(s + EPS)


def mm(a, b):
    return jnp.dot(a, b, preferred_element_type=F32)


def by_level(tokens, levels, start, count):
    rows = [pl.ds(start * LEV + l, count, stride=LEV) for l in levels]
    tiles = [jnp.concatenate([tokens[j, r] for r in rows], axis=0) for j in range(tokens.shape[0])]
    return jnp.concatenate([t.astype(BF16) for t in tiles], axis=1)


def split_tiles(tokens, v):
    for j in range(tokens.shape[0]):
        tokens[j, :v.shape[0]] = v[:, j * LANES:(j + 1) * LANES]


def gather(tokens, rows):
    return jnp.concatenate([tokens[j, rows].astype(BF16) for j in range(tokens.shape[0])], axis=1)


def attention(q, k, v, b, out, levels, start, step, used):
    count, width = q.shape
    low = lax.broadcasted_iota(jnp.int32, (count, 2 * HD), 1) < HD
    zero = jnp.zeros((count, 2 * HD), BF16)
    b = jnp.concatenate([b, b], axis=0)
    for pair in range(width // (2 * HD)):
        lanes = slice(pair * 2 * HD, (pair + 1) * 2 * HD)
        qp = q[:, lanes]
        qq = jnp.concatenate([jnp.where(low, qp, zero), jnp.where(low, zero, qp)], axis=0)
        s = lax.dot_general(
            qq, k[:, lanes], (((1,), (1,)), ((), ())), preferred_element_type=F32
        )
        s = s + b
        p = jnp.exp2(s - jnp.max(s, axis=-1, keepdims=True))
        total = jnp.sum(p, axis=-1, keepdims=True)
        o = mm(p.astype(BF16), v[:, lanes]) / total
        o = jnp.where(low, o[:count], o[count:])
        for i, l in enumerate(levels):
            out[pair, pl.ds(start * LEV + l, used, stride=LEV)] = o[i * step:i * step + used]


def kernel(
    n_lat, n_lon, x, kind, table, bias_h, cbias_h,
    wq_h, wkv_h, wo_h, w1_h, w2_h, wm_h, wc_h, wco_h,
    fine, coarse,
    bias, cbias, wq, wkv, wo, w1, w2, wm, wc, wco,
    emb, fs, q, k, v, nat, att, aft, hid, cin, cq, ck, cv, cnat, catt, cs,
    load_sem, own_sem, s1, r1, s2, r2, s3, r3, s4, r4,
):
    lat, lon = lax.axis_index("lat"), lax.axis_index("lon")
    up, down = lax.rem(lat + n_lat - 1, n_lat), lax.rem(lat + 1, n_lat)
    left, right = lax.rem(lon + n_lon - 1, n_lon), lax.rem(lon + 1, n_lon)
    rows, cols = x.shape[0], x.shape[1]

    loads = {}
    for at, (name, src, dst) in enumerate([
        ("x", x, emb.at[pl.ds(0, rows), pl.ds(0, cols)]),
        ("wq", wq_h, wq), ("wkv", wkv_h, wkv), ("bias", bias_h, bias),
        ("wo", wo_h, wo), ("w1", w1_h, w1), ("w2", w2_h, w2),
        ("wm", wm_h, wm), ("wc", wc_h, wc), ("cbias", cbias_h, cbias), ("wco", wco_h, wco),
    ]):
        loads[name] = pltpu.make_async_copy(src, dst, load_sem.at[at])

    def load(*names):
        for name in names:
            loads[name].start()

    def loaded(*names):
        for name in names:
            loads[name].wait()

    load("x", "wq", "wkv")
    places = [(up, lon), (lat, left), (up, left), (down, lon), (lat, right), (down, right)]
    barrier = pltpu.get_barrier_semaphore()
    for a, o in places:
        pl.semaphore_signal(
            barrier, inc=1, device_id={"lat": a, "lon": o}, device_id_type=pl.DeviceIdType.MESH
        )

    def send(src, dst, ssem, rsem, a, o):
        return pltpu.make_async_remote_copy(
            src_ref=src, dst_ref=dst, send_sem=ssem, recv_sem=rsem,
            device_id={"lat": a, "lon": o}, device_id_type=pl.DeviceIdType.MESH,
        )

    def part(ref, r, c):
        return ref.at[pl.ds(r[0], r[1] - r[0]), pl.ds(c[0], c[1] - c[0])]

    def shift_up(grid, pieces, ssem, rsem):
        out = []
        for at, (r, c) in enumerate(pieces):
            a, o, rr, cc = lat, lon, r, c
            if r[1] <= SR:
                a, rr = up, (r[0] + rows, r[1] + rows)
            if c[1] <= SC:
                o, cc = left, (c[0] + cols, c[1] + cols)
            out.append(send(part(grid, r, c), part(grid, rr, cc), ssem.at[at], rsem.at[at], a, o))
        return out

    def shift_down(grid, place, pieces, n_rows, n_cols, ssem, rsem):
        out = []
        for at, (r, c) in enumerate(pieces):
            a, o = lat, lon
            rr, cc = (r[0] + SR, r[1] + SR), (c[0] + SC, c[1] + SC)
            if rr[0] >= n_rows:
                a, rr = down, (rr[0] - n_rows, rr[1] - n_rows)
            if cc[0] >= n_cols:
                o, cc = right, (cc[0] - n_cols, cc[1] - n_cols)
            out.append(send(part(grid, r, c), part(place, rr, cc), ssem.at[at], rsem.at[at], a, o))
        return out

    loaded("x")
    load("bias", "wo", "w1", "w2")
    kinds = kind[...].astype(F32)
    table_rows = jnp.concatenate([table[...], jnp.zeros_like(table[:1])], axis=0).reshape(16, -1)
    band = (SR, cols * LEV, cols)
    here = lax.broadcasted_iota(jnp.int32, band, 1) // LEV == lax.broadcasted_iota(jnp.int32, band, 2)
    n_tok = SR * cols * LEV
    lane = lax.broadcasted_iota(jnp.int32, (n_tok, 16), 1)
    level = lax.broadcasted_iota(jnp.int32, (n_tok, 16), 0) % LEV
    lane_level = (lane % LEV == level)
    lane_kind = (lane // LEV).astype(F32)
    for s in range(0, rows, SR):
        spread = jnp.broadcast_to(kinds[s:s + SR][:, None, :], band)
        own = jnp.sum(jnp.where(here, spread, 0.0), axis=-1, keepdims=True).reshape(n_tok, 1)
        hot = jnp.where(lane_level & (lane_kind == own), 1.0, 0.0).astype(BF16)
        e = emb[s:s + SR, :cols].reshape(n_tok, -1).astype(F32) + mm(hot, table_rows)
        emb[s:s + SR, :cols] = e.astype(BF16).reshape(SR, cols, LEV, -1)

    pl.semaphore_wait(barrier, len(places))
    first = shift_up(
        emb, [((0, 3), (6, 18)), ((3, 9), (0, 6)), ((0, 3), (18, 24)), ((0, 3), (0, 6)), ((9, 12), (0, 6))],
        s1, r1,
    )
    for copy in first:
        copy.start()
    second = shift_up(
        fs, [((0, 3), (0, 6)), ((0, 3), (6, 12)), ((3, 6), (0, 6)), ((0, 3), (12, 24)), ((6, 12), (0, 6))],
        s2, r2,
    )
    back = shift_down(
        fs, fine,
        [((0, 6), (18, 24)), ((9, 12), (0, 12)), ((6, 9), (18, 24)), ((9, 12), (12, 18)), ((9, 12), (18, 24))],
        rows, cols, s3, r3,
    )
    keep = pltpu.make_async_copy(
        part(fs, (0, rows - SR), (0, cols - SC)), part(fine, (SR, rows), (SC, cols)), own_sem.at[0]
    )
    scale = math.log2(math.e) / math.sqrt(HD)
    loaded("wq", "wkv")

    def window(w, carry):
        wr, wc_ = w // 2, w % 2

        @pl.when(w == 1)
        def _():
            first[1].wait_recv()

        @pl.when(w == 2)
        def _():
            first[0].wait_recv()

        @pl.when(w == 3)
        def _():
            for copy in first[2:]:
                copy.wait_recv()

        e = emb[pl.ds(SR + WR * wr, WR), pl.ds(SC + WC * wc_, WC)].reshape(WIN, -1)
        aft[...] = e
        split_tiles(nat, norm(e))
        n = jnp.concatenate([by_level(nat, levels, 0, POS) for levels in GROUPS], axis=0)
        q[...] = (mm(n, wq[...]) * scale).astype(BF16)
        k[...] = mm(n, wkv[:, :512]).astype(BF16)
        v[...] = mm(n, wkv[:, 512:]).astype(BF16)
        wrapped = jnp.where((lat == n_lat - 1) & (wr == 1), 2, 0)

        @pl.when(w == 0)
        def _():
            loaded("bias")

        for g, levels in enumerate(GROUPS):
            at = pl.ds(g * GRP, GRP)
            attention(q.at[at], k.at[at], v.at[at], bias[wrapped + g], att, levels, 0, POS, POS)

        @pl.when(w == 0)
        def _():
            loaded("wo", "w1", "w2")
            load("wm", "wc", "cbias", "wco")

        a = (aft[...].astype(F32) + mm(gather(att, slice(None)), wo[...])).astype(BF16)
        aft[...] = a
        n = norm(a).astype(BF16)
        for j in range(0, 2048, 512):
            hid[:, j:j + 512] = jax.nn.gelu(mm(n, w1[:, j:j + 512])).astype(BF16)
        f = (aft[...].astype(F32) + mm(hid[...], w2[...])).astype(BF16)
        fs[pl.ds(WR * wr, WR), pl.ds(WC * wc_, WC)] = f.reshape(WR, WC, LEV, -1)

        @pl.when(w == 0)
        def _():
            for copy in second[:3]:
                copy.start()

        @pl.when(w == 1)
        def _():
            second[3].start()

        @pl.when(w == 2)
        def _():
            second[4].start()

        return carry

    lax.fori_loop(0, 4, window, 0)

    loaded("wm")
    for copy in second:
        copy.wait_recv()
    for copy in back:
        copy.start()
    keep.start()
    f = fs[pl.ds(SR, rows), pl.ds(SC, cols)].reshape(rows // 2, 2, cols // 2, 2, LEV, -1)
    m = norm(jnp.concatenate([f[:, j % 2, :, j // 2].reshape(WIN, -1) for j in range(4)], axis=1)).astype(BF16)
    for j in range(0, 1024, 512):
        cin[:, j:j + 512] = mm(m, wm[:, j:j + 512]).astype(BF16)
    split_tiles(cnat, norm(cin[...]))
    cnat[:, WIN:] = jnp.zeros_like(cnat[:, WIN:])
    nk = jnp.concatenate([by_level(cnat, levels, 0, POS) for levels in GROUPS], axis=0)
    nq = [by_level(cnat, levels, h * POS // 2, QPAD) for h in range(2) for levels in GROUPS]
    nq = jnp.concatenate(nq, axis=0)
    loaded("wc", "cbias", "wco")
    for j in range(0, 1024, 512):
        cq[:, j:j + 512] = (mm(nq, wc[:, j:j + 512]) * scale).astype(BF16)
        ck[:, j:j + 512] = mm(nk, wc[:, 1024 + j:1536 + j]).astype(BF16)
        cv[:, j:j + 512] = mm(nk, wc[:, 2048 + j:2560 + j]).astype(BF16)
    wrapped = jnp.where(lat == n_lat - 1, 4, 0)
    third = shift_down(
        cs, coarse, [((3, 6), (0, 6)), ((3, 6), (6, 12)), ((0, 3), (6, 12))], WR, WC, s4, r4
    )
    keep_too = pltpu.make_async_copy(
        part(cs, (0, SR), (0, SC)), part(coarse, (SR, WR), (SC, WC)), own_sem.at[1]
    )
    for half in (1, 0):
        for g, levels in enumerate(GROUPS):
            at = pl.ds((half * 2 + g) * 2 * QPAD, 2 * QPAD)
            keys = pl.ds(g * GRP, GRP)
            attention(
                cq.at[at], ck.at[keys], cv.at[keys], cbias[wrapped + g * 2 + half],
                catt, levels, half * POS // 2, QPAD, POS // 2,
            )
        mixed = gather(catt, slice(half * GRP, (half + 1) * GRP))
        at = slice(half * GRP, (half + 1) * GRP)
        for j in range(0, 1024, 512):
            t = (cin[at, j:j + 512].astype(F32) + mm(mixed, wco[:, j:j + 512])).astype(BF16)
            cs[half * SR:(half + 1) * SR, :, :, j:j + 512] = t.reshape(SR, WC, LEV, -1)
        if half == 1:
            third[0].start()
            third[1].start()
        else:
            third[2].start()
            keep_too.start()
    for copy in back + third:
        copy.wait_recv()
    keep.wait()
    keep_too.wait()
    for copy in first + second + back + third:
        copy.wait_send()


def local(
    n_lat, n_lon, tokens, surface_kind, kind_table, attn_q_w, attn_kv_w, attn_out_w,
    mlp_in_w, mlp_out_w, merge_w, coarse_qkv_w, coarse_out_w,
):
    rows, cols, lev, width = tokens.shape
    consts = [jnp.asarray(a) for a in biases()]
    weights = [attn_q_w, attn_kv_w, attn_out_w, mlp_in_w, mlp_out_w, merge_w, coarse_qkv_w, coarse_out_w]
    vmem, hbm = pl.BlockSpec(memory_space=pltpu.VMEM), pl.BlockSpec(memory_space=pl.ANY)
    dma = pltpu.SemaphoreType.DMA
    buf = lambda *shape: pltpu.VMEM(shape, BF16)
    frame = buf(rows + SR, cols + SC, lev, width)
    return pl.pallas_call(
        functools.partial(kernel, n_lat, n_lon),
        out_shape=(
            buf(rows, cols, lev, width),
            buf(rows // 2, cols // 2, lev, 2 * width),
        ),
        in_specs=[hbm, vmem, vmem] + [hbm] * 10,
        out_specs=(hbm, hbm),
        scratch_shapes=[
            *[pltpu.VMEM(a.shape, a.dtype) for a in consts + weights],
            frame, frame, *[buf(WIN, width)] * 3, *[pltpu.VMEM((width // LANES, WIN, LANES), F32)] * 2, buf(WIN, width),
            buf(WIN, 4 * width),
            buf(WIN, 2 * width), buf(8 * QPAD, 2 * width), buf(WIN, 2 * width), buf(WIN, 2 * width),
            pltpu.VMEM((2 * width // LANES, WIN + LEV * (2 * QPAD - POS), LANES), F32),
            pltpu.VMEM((2 * width // LANES, WIN, LANES), F32),
            buf(WR, WC, lev, 2 * width),
            dma((11,)), dma((2,)), dma((5,)), dma((5,)), dma((5,)), dma((5,)), dma((5,)), dma((5,)),
            dma((3,)), dma((3,)),
        ],
        compiler_params=pltpu.CompilerParams(
            collective_id=0, has_side_effects=True, vmem_limit_bytes=60 * 1024 * 1024
        ),
        name="block",
    )(tokens, surface_kind, kind_table, *consts, *weights)


def solution(mesh):
    grid = P("lat", "lon", None, None)
    return jax.shard_map(
        functools.partial(local, mesh.shape["lat"], mesh.shape["lon"]),
        mesh=mesh,
        in_specs=(grid, P("lat", "lon")) + (P(),) * 9,
        out_specs=(grid, grid),
        check_vma=False,
    )
```

time: 50.1 us -> 48 us (0.958)
  the two profiles are of different devices: /device:TPU:1 before, /device:TPU:0 now
where the time goes in v3:
time: 48 us; the launch traced here: 47.8 us
  Pallas kernels  45.4 us (95%)
  local copies, waits for them, and re-layouts  1.83 us (4%)
  between operations  0.64 us (1%)
    pallas_call x1, Pallas kernels, local(): pl.pallas_call(functools.partial(kernel, n_lat, n_lon), out_shape=(buf(ro...  45.4 us
    unnamed x2, local copies, waits for them, and re-layouts  1.83 us

profile of v3, /device:TPU:0, one launch (start us, length us, event | category | flops | bytes accessed | tf_op | source)
XLA Modules:
  0.0 47.8 jit_solution(18095891404981509417)
XLA Ops:
  0.6 45.4 %block.1 = (bf16[12,24,4,512]{3,2,1,0:T(4,128)(2,1)S(1)}, bf16[6,12,4,1024]{3,2,1,0:T(4,128)(2,1)S(1)}) custom-call(bf16[12,24,4,512]{3,2,1,0:T(4,128)(2,1)} %x.1, s32[12,24]{1,0:T(8,128)} %kind.1, bf16[3,4,512]{2,1,0:T(4,128)(2,1)} %table.1, f32[4,144,144]{2,1,0:T(8,128)} %constant.4.clone.bias_h, f32[8,80,144]{2,1,0:T(8,128)} %constant.5.clone.cbias_h, ...), custom_call_target="tpu_custom_call" | custom-call | tf_op jit(solution)/shard_map/block/pallas_call | solution.py:325
  46.0 1.0 %copy.17 = bf16[12,24,4,512]{3,2,1,0:T(4,128)(2,1)} copy(bf16[12,24,4,512]{3,2,1,0:T(4,128)(2,1)S(1)} %get-tuple-element.2) | data formatting | bytes 2359296
  47.0 0.8 %copy.18 = bf16[6,12,4,1024]{3,2,1,0:T(4,128)(2,1)} copy(bf16[6,12,4,1024]{3,2,1,0:T(4,128)(2,1)S(1)} %get-tuple-element.3) | data formatting | bytes 1179648

commit v4 on v3

--- a/solution.py
+++ b/solution.py
@@ -42,6 +42,11 @@
     c = v - jnp.mean(v, axis=-1, keepdims=True)
     s = jnp.mean(c * c, axis=-1, keepdims=True)
     return c * lax.rsqrt(s + EPS)
+
+
+def gelu(x):
+    inner = x * (math.sqrt(2 / math.pi) + math.sqrt(2 / math.pi) * 0.044715 * (x * x))
+    return 0.5 * x * (1.0 + jnp.tanh(inner))
 
 
 def mm(a, b):
@@ -82,14 +87,15 @@
         o = jnp.where(low, o[:count], o[count:])
         for i, l in enumerate(levels):
             out[pair, pl.ds(start * LEV + l, used, stride=LEV)] = o[i * step:i * step + used]
+        yield
 
 
 def kernel(
-    n_lat, n_lon, x, kind, table, bias_h, cbias_h,
+    n_lat, n_lon, x, kind_h, table_h, bias_h, cbias_h,
     wq_h, wkv_h, wo_h, w1_h, w2_h, wm_h, wc_h, wco_h,
     fine, coarse,
-    bias, cbias, wq, wkv, wo, w1, w2, wm, wc, wco,
-    emb, fs, q, k, v, nat, att, aft, hid, cin, cq, ck, cv, cnat, catt, cs,
+    kind, table, bias, cbias, wq, wkv, wo, w1, w2, wm, wc, wco,
+    emb, fs, q, k, v, nat, att, aft, done, hid, cin, cq, ck, cv, cnat, catt, cs,
     load_sem, own_sem, s1, r1, s2, r2, s3, r3, s4, r4,
 ):
     lat, lon = lax.axis_index("lat"), lax.axis_index("lon")
@@ -97,24 +103,6 @@
     left, right = lax.rem(lon + n_lon - 1, n_lon), lax.rem(lon + 1, n_lon)
     rows, cols = x.shape[0], x.shape[1]
 
-    loads = {}
-    for at, (name, src, dst) in enumerate([
-        ("x", x, emb.at[pl.ds(0, rows), pl.ds(0, cols)]),
-        ("wq", wq_h, wq), ("wkv", wkv_h, wkv), ("bias", bias_h, bias),
-        ("wo", wo_h, wo), ("w1", w1_h, w1), ("w2", w2_h, w2),
-        ("wm", wm_h, wm), ("wc", wc_h, wc), ("cbias", cbias_h, cbias), ("wco", wco_h, wco),
-    ]):
-        loads[name] = pltpu.make_async_copy(src, dst, load_sem.at[at])
-
-    def load(*names):
-        for name in names:
-            loads[name].start()
-
-    def loaded(*names):
-        for name in names:
-            loads[name].wait()
-
-    load("x", "wq", "wkv")
     places = [(up, lon), (lat, left), (up, left), (down, lon), (lat, right), (down, right)]
     barrier = pltpu.get_barrier_semaphore()
     for a, o in places:
@@ -122,6 +110,24 @@
             barrier, inc=1, device_id={"lat": a, "lon": o}, device_id_type=pl.DeviceIdType.MESH
         )
 
+    loads = {}
+    for at, (name, src, dst) in enumerate([
+        ("kind", kind_h, kind), ("table", table_h, table), ("x", x, emb.at[pl.ds(0, rows), pl.ds(0, cols)]),
+        ("wq", wq_h, wq), ("wkv", wkv_h, wkv), ("bias", bias_h, bias),
+        ("wo", wo_h, wo), ("w1", w1_h, w1), ("w2", w2_h, w2),
+        ("wm", wm_h, wm), ("wc", wc_h, wc), ("cbias", cbias_h, cbias), ("wco", wco_h, wco),
+    ]):
+        loads[name] = pltpu.make_async_copy(src, dst, load_sem.at[at])
+
+    def load(*names):
+        for name in names:
+            loads[name].start()
+
+    def loaded(*names):
+        for name in names:
+            loads[name].wait()
+
+    load("kind", "table", "x", "wq", "wkv")
     def send(src, dst, ssem, rsem, a, o):
         return pltpu.make_async_remote_copy(
             src_ref=src, dst_ref=dst, send_sem=ssem, recv_sem=rsem,
@@ -154,7 +160,12 @@
             out.append(send(part(grid, r, c), part(place, rr, cc), ssem.at[at], rsem.at[at], a, o))
         return out
 
-    loaded("x")
+    first = shift_up(
+        emb, [((0, 3), (6, 18)), ((3, 9), (0, 6)), ((0, 3), (18, 24)), ((0, 3), (0, 6)), ((9, 12), (0, 6))],
+        s1, r1,
+    )
+
+    loaded("kind", "table", "x")
     load("bias", "wo", "w1", "w2")
     kinds = kind[...].astype(F32)
     table_rows = jnp.concatenate([table[...], jnp.zeros_like(table[:1])], axis=0).reshape(16, -1)
@@ -171,14 +182,12 @@
         hot = jnp.where(lane_level & (lane_kind == own), 1.0, 0.0).astype(BF16)
         e = emb[s:s + SR, :cols].reshape(n_tok, -1).astype(F32) + mm(hot, table_rows)
         emb[s:s + SR, :cols] = e.astype(BF16).reshape(SR, cols, LEV, -1)
-
-    pl.semaphore_wait(barrier, len(places))
-    first = shift_up(
-        emb, [((0, 3), (6, 18)), ((3, 9), (0, 6)), ((0, 3), (18, 24)), ((0, 3), (0, 6)), ((9, 12), (0, 6))],
-        s1, r1,
-    )
-    for copy in first:
-        copy.start()
+        if s == 0:
+            pl.semaphore_wait(barrier, len(places))
+            for at in (0, 2, 3):
+                first[at].start()
+    first[1].start()
+    first[4].start()
     second = shift_up(
         fs, [((0, 3), (0, 6)), ((0, 3), (6, 12)), ((3, 6), (0, 6)), ((0, 3), (12, 24)), ((6, 12), (0, 6))],
         s2, r2,
@@ -194,75 +203,82 @@
     scale = math.log2(math.e) / math.sqrt(HD)
     loaded("wq", "wkv")
 
-    def window(w, carry):
+    def front(w):
         wr, wc_ = w // 2, w % 2
-
-        @pl.when(w == 1)
-        def _():
-            first[1].wait_recv()
-
-        @pl.when(w == 2)
-        def _():
-            first[0].wait_recv()
-
-        @pl.when(w == 3)
-        def _():
-            for copy in first[2:]:
-                copy.wait_recv()
-
         e = emb[pl.ds(SR + WR * wr, WR), pl.ds(SC + WC * wc_, WC)].reshape(WIN, -1)
         aft[...] = e
         split_tiles(nat, norm(e))
+        yield
         n = jnp.concatenate([by_level(nat, levels, 0, POS) for levels in GROUPS], axis=0)
         q[...] = (mm(n, wq[...]) * scale).astype(BF16)
+        yield
         k[...] = mm(n, wkv[:, :512]).astype(BF16)
+        yield
         v[...] = mm(n, wkv[:, 512:]).astype(BF16)
+        yield
         wrapped = jnp.where((lat == n_lat - 1) & (wr == 1), 2, 0)
-
-        @pl.when(w == 0)
-        def _():
-            loaded("bias")
-
         for g, levels in enumerate(GROUPS):
             at = pl.ds(g * GRP, GRP)
-            attention(q.at[at], k.at[at], v.at[at], bias[wrapped + g], att, levels, 0, POS, POS)
-
-        @pl.when(w == 0)
-        def _():
-            loaded("wo", "w1", "w2")
-            load("wm", "wc", "cbias", "wco")
-
+            for _ in attention(q.at[at], k.at[at], v.at[at], bias[wrapped + g], att, levels, 0, POS, POS):
+                yield
         a = (aft[...].astype(F32) + mm(gather(att, slice(None)), wo[...])).astype(BF16)
-        aft[...] = a
-        n = norm(a).astype(BF16)
+        yield
+        done[...] = a
+
+    def back_half(w):
+        wr, wc_ = w // 2, w % 2
+        n = norm(done[...]).astype(BF16)
+        yield
         for j in range(0, 2048, 512):
-            hid[:, j:j + 512] = jax.nn.gelu(mm(n, w1[:, j:j + 512])).astype(BF16)
-        f = (aft[...].astype(F32) + mm(hid[...], w2[...])).astype(BF16)
-        fs[pl.ds(WR * wr, WR), pl.ds(WC * wc_, WC)] = f.reshape(WR, WC, LEV, -1)
-
-        @pl.when(w == 0)
+            hid[:, j:j + 512] = gelu(mm(n, w1[:, j:j + 512])).astype(BF16)
+            yield
+        for j in range(0, 512, 256):
+            f = (done[:, j:j + 256].astype(F32) + mm(hid[...], w2[:, j:j + 256])).astype(BF16)
+            fs[pl.ds(WR * wr, WR), pl.ds(WC * wc_, WC), :, j:j + 256] = f.reshape(WR, WC, LEV, -1)
+            yield
+
+    def window(w, carry):
+        for _ in back_half(w - 1):
+            pass
+
+        @pl.when(w == 1)
         def _():
             for copy in second[:3]:
                 copy.start()
-
-        @pl.when(w == 1)
+            first[1].wait_recv()
+
+        @pl.when(w == 2)
         def _():
             second[3].start()
-
-        @pl.when(w == 2)
+            first[0].wait_recv()
+
+        @pl.when(w == 3)
         def _():
             second[4].start()
-
+            back[0].start()
+            back[1].start()
+            for copy in first[2:]:
+                copy.wait_recv()
+
+        for _ in front(w):
+            pass
         return carry
 
-    lax.fori_loop(0, 4, window, 0)
+    loaded("bias", "wo")
+    for _ in front(0):
+        pass
+    loaded("w1", "w2")
+    load("wm", "wc", "cbias", "wco")
+    lax.fori_loop(1, 4, window, 0)
+    for _ in back_half(3):
+        pass
+    for copy in back[2:]:
+        copy.start()
+    keep.start()
 
     loaded("wm")
     for copy in second:
         copy.wait_recv()
-    for copy in back:
-        copy.start()
-    keep.start()
     f = fs[pl.ds(SR, rows), pl.ds(SC, cols)].reshape(rows // 2, 2, cols // 2, 2, LEV, -1)
     m = norm(jnp.concatenate([f[:, j % 2, :, j // 2].reshape(WIN, -1) for j in range(4)], axis=1)).astype(BF16)
     for j in range(0, 1024, 512):
@@ -270,11 +286,8 @@
     split_tiles(cnat, norm(cin[...]))
     cnat[:, WIN:] = jnp.zeros_like(cnat[:, WIN:])
     nk = jnp.concatenate([by_level(cnat, levels, 0, POS) for levels in GROUPS], axis=0)
-    nq = [by_level(cnat, levels, h * POS // 2, QPAD) for h in range(2) for levels in GROUPS]
-    nq = jnp.concatenate(nq, axis=0)
     loaded("wc", "cbias", "wco")
     for j in range(0, 1024, 512):
-        cq[:, j:j + 512] = (mm(nq, wc[:, j:j + 512]) * scale).astype(BF16)
         ck[:, j:j + 512] = mm(nk, wc[:, 1024 + j:1536 + j]).astype(BF16)
         cv[:, j:j + 512] = mm(nk, wc[:, 2048 + j:2560 + j]).astype(BF16)
     wrapped = jnp.where(lat == n_lat - 1, 4, 0)
@@ -285,13 +298,18 @@
         part(cs, (0, SR), (0, SC)), part(coarse, (SR, WR), (SC, WC)), own_sem.at[1]
     )
     for half in (1, 0):
+        nq = [by_level(cnat, levels, half * POS // 2, QPAD) for levels in GROUPS]
+        nq = jnp.concatenate(nq, axis=0)
+        for j in range(0, 1024, 512):
+            cq[:, j:j + 512] = (mm(nq, wc[:, j:j + 512]) * scale).astype(BF16)
         for g, levels in enumerate(GROUPS):
-            at = pl.ds((half * 2 + g) * 2 * QPAD, 2 * QPAD)
+            at = pl.ds(g * 2 * QPAD, 2 * QPAD)
             keys = pl.ds(g * GRP, GRP)
-            attention(
+            for _ in attention(
                 cq.at[at], ck.at[keys], cv.at[keys], cbias[wrapped + g * 2 + half],
                 catt, levels, half * POS // 2, QPAD, POS // 2,
-            )
+            ):
+                pass
         mixed = gather(catt, slice(half * GRP, (half + 1) * GRP))
         at = slice(half * GRP, (half + 1) * GRP)
         for j in range(0, 1024, 512):
@@ -318,7 +336,7 @@
     rows, cols, lev, width = tokens.shape
     consts = [jnp.asarray(a) for a in biases()]
     weights = [attn_q_w, attn_kv_w, attn_out_w, mlp_in_w, mlp_out_w, merge_w, coarse_qkv_w, coarse_out_w]
-    vmem, hbm = pl.BlockSpec(memory_space=pltpu.VMEM), pl.BlockSpec(memory_space=pl.ANY)
+    hbm = pl.BlockSpec(memory_space=pl.ANY)
     dma = pltpu.SemaphoreType.DMA
     buf = lambda *shape: pltpu.VMEM(shape, BF16)
     frame = buf(rows + SR, cols + SC, lev, width)
@@ -328,17 +346,18 @@
             buf(rows, cols, lev, width),
             buf(rows // 2, cols // 2, lev, 2 * width),
         ),
-        in_specs=[hbm, vmem, vmem] + [hbm] * 10,
+        in_specs=[hbm] * 13,
         out_specs=(hbm, hbm),
         scratch_shapes=[
-            *[pltpu.VMEM(a.shape, a.dtype) for a in consts + weights],
-            frame, frame, *[buf(WIN, width)] * 3, *[pltpu.VMEM((width // LANES, WIN, LANES), F32)] * 2, buf(WIN, width),
+            *[pltpu.VMEM(a.shape, a.dtype) for a in [surface_kind, kind_table] + consts + weights],
+            frame, frame, *[buf(WIN, width)] * 3, *[pltpu.VMEM((width // LANES, WIN, LANES), F32)] * 2,
+            buf(WIN, width), buf(WIN, width),
             buf(WIN, 4 * width),
-            buf(WIN, 2 * width), buf(8 * QPAD, 2 * width), buf(WIN, 2 * width), buf(WIN, 2 * width),
+            buf(WIN, 2 * width), buf(4 * QPAD, 2 * width), buf(WIN, 2 * width), buf(WIN, 2 * width),
             pltpu.VMEM((2 * width // LANES, WIN + LEV * (2 * QPAD - POS), LANES), F32),
             pltpu.VMEM((2 * width // LANES, WIN, LANES), F32),
             buf(WR, WC, lev, 2 * width),
-            dma((11,)), dma((2,)), dma((5,)), dma((5,)), dma((5,)), dma((5,)), dma((5,)), dma((5,)),
+            dma((13,)), dma((2,)), dma((5,)), dma((5,)), dma((5,)), dma((5,)), dma((5,)), dma((5,)),
             dma((3,)), dma((3,)),
         ],
         compiler_params=pltpu.CompilerParams(

time: 48 us -> 46.6 us (0.971)
  Pallas kernels: 45.4 us -> 43.9 us
    pallas_call x1, Pallas kernels: 45.4 us -> 43.9 us  [local(): pl.pallas_call(functools.partial(kernel, n_lat, n_lon), out_shape=(buf(ro...]
where the time goes in v4:
time: 46.6 us; the launch traced here: 46.4 us
  Pallas kernels  43.9 us (94%)
  local copies, waits for them, and re-layouts  1.83 us (4%)
  between operations  0.64 us (1%)
    pallas_call x1, Pallas kernels, local(): pl.pallas_call(functools.partial(kernel, n_lat, n_lon), out_shape=(buf(ro...  43.9 us
    unnamed x2, local copies, waits for them, and re-layouts  1.83 us

profile of v4, /device:TPU:0, one launch (start us, length us, event | category | flops | bytes accessed | tf_op | source)
XLA Modules:
  0.0 46.4 jit_solution(17692787259504815349)
XLA Ops:
  0.6 43.9 %block.1 = (bf16[12,24,4,512]{3,2,1,0:T(4,128)(2,1)S(1)}, bf16[6,12,4,1024]{3,2,1,0:T(4,128)(2,1)S(1)}) custom-call(bf16[12,24,4,512]{3,2,1,0:T(4,128)(2,1)} %x.1, s32[12,24]{1,0:T(8,128)} %kind_h.1, bf16[3,4,512]{2,1,0:T(4,128)(2,1)} %table_h.1, f32[4,144,144]{2,1,0:T(8,128)} %constant.4.clone.bias_h, f32[8,80,144]{2,1,0:T(8,128)} %constant.5.clone.cbias_h, ...), custom_call_target="tpu_custom_call" | custom-call | tf_op jit(solution)/shard_map/block/pallas_call | solution.py:343
  44.6 1.0 %copy.17 = bf16[12,24,4,512]{3,2,1,0:T(4,128)(2,1)} copy(bf16[12,24,4,512]{3,2,1,0:T(4,128)(2,1)S(1)} %get-tuple-element.2) | data formatting | bytes 2359296
  45.6 0.8 %copy.18 = bf16[6,12,4,1024]{3,2,1,0:T(4,128)(2,1)} copy(bf16[6,12,4,1024]{3,2,1,0:T(4,128)(2,1)S(1)} %get-tuple-element.3) | data formatting | bytes 1179648

commit v5 on v4

--- a/solution.py
+++ b/solution.py
@@ -103,7 +103,7 @@
     left, right = lax.rem(lon + n_lon - 1, n_lon), lax.rem(lon + 1, n_lon)
     rows, cols = x.shape[0], x.shape[1]
 
-    places = [(up, lon), (lat, left), (up, left), (down, lon), (lat, right), (down, right)]
+    places = [(down, lon), (lat, right), (down, right)]
     barrier = pltpu.get_barrier_semaphore()
     for a, o in places:
         pl.semaphore_signal(
@@ -184,10 +184,8 @@
         emb[s:s + SR, :cols] = e.astype(BF16).reshape(SR, cols, LEV, -1)
         if s == 0:
             pl.semaphore_wait(barrier, len(places))
-            for at in (0, 2, 3):
-                first[at].start()
+            first[0].start()
     first[1].start()
-    first[4].start()
     second = shift_up(
         fs, [((0, 3), (0, 6)), ((0, 3), (6, 12)), ((3, 6), (0, 6)), ((0, 3), (12, 24)), ((6, 12), (0, 6))],
         s2, r2,
@@ -256,7 +254,6 @@
         def _():
             second[4].start()
             back[0].start()
-            back[1].start()
             for copy in first[2:]:
                 copy.wait_recv()
 
@@ -267,9 +264,12 @@
     loaded("bias", "wo")
     for _ in front(0):
         pass
+    for copy in first[2:]:
+        copy.start()
     loaded("w1", "w2")
     load("wm", "wc", "cbias", "wco")
     lax.fori_loop(1, 4, window, 0)
+    back[1].start()
     for _ in back_half(3):
         pass
     for copy in back[2:]:

time: 46.6 us -> 46 us (0.987)
  Pallas kernels: 43.9 us -> 43.4 us
    pallas_call x1, Pallas kernels: 43.9 us -> 43.4 us  [local(): pl.pallas_call(functools.partial(kernel, n_lat, n_lon), out_shape=(buf(ro...]
where the time goes in v5:
time: 46 us; the launch traced here: 45.8 us
  Pallas kernels  43.4 us (94%)
  local copies, waits for them, and re-layouts  1.83 us (4%)
  between operations  0.64 us (1%)
    pallas_call x1, Pallas kernels, local(): pl.pallas_call(functools.partial(kernel, n_lat, n_lon), out_shape=(buf(ro...  43.4 us
    unnamed x2, local copies, waits for them, and re-layouts  1.83 us

profile of v5, /device:TPU:0, one launch (start us, length us, event | category | flops | bytes accessed | tf_op | source)
XLA Modules:
  0.0 45.8 jit_solution(413676428502708191)
XLA Ops:
  0.6 43.4 %block.1 = (bf16[12,24,4,512]{3,2,1,0:T(4,128)(2,1)S(1)}, bf16[6,12,4,1024]{3,2,1,0:T(4,128)(2,1)S(1)}) custom-call(bf16[12,24,4,512]{3,2,1,0:T(4,128)(2,1)} %x.1, s32[12,24]{1,0:T(8,128)} %kind_h.1, bf16[3,4,512]{2,1,0:T(4,128)(2,1)} %table_h.1, f32[4,144,144]{2,1,0:T(8,128)} %constant.4.clone.bias_h, f32[8,80,144]{2,1,0:T(8,128)} %constant.5.clone.cbias_h, ...), custom_call_target="tpu_custom_call" | custom-call | tf_op jit(solution)/shard_map/block/pallas_call | solution.py:343
  44.0 1.0 %copy.17 = bf16[12,24,4,512]{3,2,1,0:T(4,128)(2,1)} copy(bf16[12,24,4,512]{3,2,1,0:T(4,128)(2,1)S(1)} %get-tuple-element.2) | data formatting | bytes 2359296
  45.0 0.8 %copy.18 = bf16[6,12,4,1024]{3,2,1,0:T(4,128)(2,1)} copy(bf16[6,12,4,1024]{3,2,1,0:T(4,128)(2,1)S(1)} %get-tuple-element.3) | data formatting | bytes 1179648

commit v6 on v5

--- a/solution.py
+++ b/solution.py
@@ -27,13 +27,17 @@
 def biases():
     at = np.arange(GRP)
     level = at // POS
-    half = at % POS // (POS // 2)
-    same_level = level[:, None] == level[None, :]
-    same_half = half[:, None] == half[None, :]
-    ok = [same_level, np.ones_like(same_level), same_level & same_half, same_half]
-    full = np.where(np.stack(ok), 0.0, -1e30).astype(np.float32)
+
+    def masks(half):
+        same_level = level[:, None] == level[None, :]
+        same_half = half[:, None] == half[None, :]
+        ok = [same_level, np.ones_like(same_level), same_level & same_half, same_half]
+        return np.where(np.stack(ok), 0.0, -1e30).astype(np.float32)
+
+    full = masks(at % POS // (POS // 2))
+    coarse = masks(at % WR // SR)
     halves = np.zeros((4, 2, 2, QPAD, GRP), np.float32)
-    halves[:, :, :, :POS // 2] = full.reshape(4, 2, 2, POS // 2, GRP).transpose(0, 2, 1, 3, 4)
+    halves[:, :, :, :POS // 2] = coarse.reshape(4, 2, 2, POS // 2, GRP).transpose(0, 2, 1, 3, 4)
     return full, halves.reshape(8, 2 * QPAD, GRP)
 
 
@@ -280,7 +284,8 @@
     for copy in second:
         copy.wait_recv()
     f = fs[pl.ds(SR, rows), pl.ds(SC, cols)].reshape(rows // 2, 2, cols // 2, 2, LEV, -1)
-    m = norm(jnp.concatenate([f[:, j % 2, :, j // 2].reshape(WIN, -1) for j in range(4)], axis=1)).astype(BF16)
+    f = [jnp.swapaxes(f[:, j % 2, :, j // 2], 0, 1).reshape(WIN, -1) for j in range(4)]
+    m = norm(jnp.concatenate(f, axis=1)).astype(BF16)
     for j in range(0, 1024, 512):
         cin[:, j:j + 512] = mm(m, wm[:, j:j + 512]).astype(BF16)
     split_tiles(cnat, norm(cin[...]))
@@ -292,7 +297,7 @@
         cv[:, j:j + 512] = mm(nk, wc[:, 2048 + j:2560 + j]).astype(BF16)
     wrapped = jnp.where(lat == n_lat - 1, 4, 0)
     third = shift_down(
-        cs, coarse, [((3, 6), (0, 6)), ((3, 6), (6, 12)), ((0, 3), (6, 12))], WR, WC, s4, r4
+        cs, coarse, [((3, 6), (6, 12)), ((0, 3), (6, 12)), ((3, 6), (0, 6))], WR, WC, s4, r4
     )
     keep_too = pltpu.make_async_copy(
         part(cs, (0, SR), (0, SC)), part(coarse, (SR, WR), (SC, WC)), own_sem.at[1]
@@ -314,7 +319,8 @@
         at = slice(half * GRP, (half + 1) * GRP)
         for j in range(0, 1024, 512):
             t = (cin[at, j:j + 512].astype(F32) + mm(mixed, wco[:, j:j + 512])).astype(BF16)
-            cs[half * SR:(half + 1) * SR, :, :, j:j + 512] = t.reshape(SR, WC, LEV, -1)
+            t = jnp.swapaxes(t.reshape(SC, WR, LEV, -1), 0, 1)
+            cs[:, half * SC:(half + 1) * SC, :, j:j + 512] = t
         if half == 1:
             third[0].start()
             third[1].start()

time: 46 us -> 46 us (level)
  no operation moved by 1% of the time
where the time goes in v6:
time: 46 us; the launch traced here: 45.9 us
  Pallas kernels  43.4 us (94%)
  local copies, waits for them, and re-layouts  1.83 us (4%)
  between operations  0.64 us (1%)
    pallas_call x1, Pallas kernels, local(): pl.pallas_call(functools.partial(kernel, n_lat, n_lon), out_shape=(buf(ro...  43.4 us
    unnamed x2, local copies, waits for them, and re-layouts  1.83 us

profile of v6, /device:TPU:0, one launch (start us, length us, event | category | flops | bytes accessed | tf_op | source)
XLA Modules:
  0.0 45.9 jit_solution(15381851916111531708)
XLA Ops:
  0.6 43.4 %block.1 = (bf16[12,24,4,512]{3,2,1,0:T(4,128)(2,1)S(1)}, bf16[6,12,4,1024]{3,2,1,0:T(4,128)(2,1)S(1)}) custom-call(bf16[12,24,4,512]{3,2,1,0:T(4,128)(2,1)} %x.1, s32[12,24]{1,0:T(8,128)} %kind_h.1, bf16[3,4,512]{2,1,0:T(4,128)(2,1)} %table_h.1, f32[4,144,144]{2,1,0:T(8,128)} %constant.4.clone.bias_h, f32[8,80,144]{2,1,0:T(8,128)} %constant.5.clone.cbias_h, ...), custom_call_target="tpu_custom_call" | custom-call | tf_op jit(solution)/shard_map/block/pallas_call | solution.py:349
  44.1 1.0 %copy.17 = bf16[12,24,4,512]{3,2,1,0:T(4,128)(2,1)} copy(bf16[12,24,4,512]{3,2,1,0:T(4,128)(2,1)S(1)} %get-tuple-element.2) | data formatting | bytes 2359296
  45.1 0.8 %copy.18 = bf16[6,12,4,1024]{3,2,1,0:T(4,128)(2,1)} copy(bf16[6,12,4,1024]{3,2,1,0:T(4,128)(2,1)S(1)} %get-tuple-element.3) | data formatting | bytes 1179648

commit v7 on v6

--- a/solution.py
+++ b/solution.py
@@ -103,11 +103,11 @@
     load_sem, own_sem, s1, r1, s2, r2, s3, r3, s4, r4,
 ):
     lat, lon = lax.axis_index("lat"), lax.axis_index("lon")
-    up, down = lax.rem(lat + n_lat - 1, n_lat), lax.rem(lat + 1, n_lat)
-    left, right = lax.rem(lon + n_lon - 1, n_lon), lax.rem(lon + 1, n_lon)
+    lat_from, lat_to = lax.rem(lat + n_lat - 1, n_lat), lax.rem(lat + 1, n_lat)
+    lon_from, lon_to = lax.rem(lon + n_lon - 1, n_lon), lax.rem(lon + 1, n_lon)
     rows, cols = x.shape[0], x.shape[1]
 
-    places = [(down, lon), (lat, right), (down, right)]
+    places = [(lat_from, lon), (lat, lon_from), (lat_from, lon_from)]
     barrier = pltpu.get_barrier_semaphore()
     for a, o in places:
         pl.semaphore_signal(
@@ -116,7 +116,7 @@
 
     loads = {}
     for at, (name, src, dst) in enumerate([
-        ("kind", kind_h, kind), ("table", table_h, table), ("x", x, emb.at[pl.ds(0, rows), pl.ds(0, cols)]),
+        ("kind", kind_h, kind), ("table", table_h, table), ("x", x, emb.at[pl.ds(SR, rows), pl.ds(SC, cols)]),
         ("wq", wq_h, wq), ("wkv", wkv_h, wkv), ("bias", bias_h, bias),
         ("wo", wo_h, wo), ("w1", w1_h, w1), ("w2", w2_h, w2),
         ("wm", wm_h, wm), ("wc", wc_h, wc), ("cbias", cbias_h, cbias), ("wco", wco_h, wco),
@@ -139,32 +139,33 @@
         )
 
     def part(ref, r, c):
-        return ref.at[pl.ds(r[0], r[1] - r[0]), pl.ds(c[0], c[1] - c[0])]
-
-    def shift_up(grid, pieces, ssem, rsem):
+        r0, c0 = ref.shape[0] - r[1], ref.shape[1] - c[1]
+        return ref.at[pl.ds(r0, r[1] - r[0]), pl.ds(c0, c[1] - c[0])]
+
+    def forward(grid, pieces, ssem, rsem):
         out = []
         for at, (r, c) in enumerate(pieces):
             a, o, rr, cc = lat, lon, r, c
             if r[1] <= SR:
-                a, rr = up, (r[0] + rows, r[1] + rows)
+                a, rr = lat_to, (r[0] + rows, r[1] + rows)
             if c[1] <= SC:
-                o, cc = left, (c[0] + cols, c[1] + cols)
+                o, cc = lon_to, (c[0] + cols, c[1] + cols)
             out.append(send(part(grid, r, c), part(grid, rr, cc), ssem.at[at], rsem.at[at], a, o))
         return out
 
-    def shift_down(grid, place, pieces, n_rows, n_cols, ssem, rsem):
+    def backward(grid, place, pieces, n_rows, n_cols, ssem, rsem):
         out = []
         for at, (r, c) in enumerate(pieces):
             a, o = lat, lon
             rr, cc = (r[0] + SR, r[1] + SR), (c[0] + SC, c[1] + SC)
             if rr[0] >= n_rows:
-                a, rr = down, (rr[0] - n_rows, rr[1] - n_rows)
+                a, rr = lat_from, (rr[0] - n_rows, rr[1] - n_rows)
             if cc[0] >= n_cols:
-                o, cc = right, (cc[0] - n_cols, cc[1] - n_cols)
+                o, cc = lon_from, (cc[0] - n_cols, cc[1] - n_cols)
             out.append(send(part(grid, r, c), part(place, rr, cc), ssem.at[at], rsem.at[at], a, o))
         return out
 
-    first = shift_up(
+    first = forward(
         emb, [((0, 3), (6, 18)), ((3, 9), (0, 6)), ((0, 3), (18, 24)), ((0, 3), (0, 6)), ((9, 12), (0, 6))],
         s1, r1,
     )
@@ -180,21 +181,21 @@
     level = lax.broadcasted_iota(jnp.int32, (n_tok, 16), 0) % LEV
     lane_level = (lane % LEV == level)
     lane_kind = (lane // LEV).astype(F32)
-    for s in range(0, rows, SR):
+    for s in reversed(range(0, rows, SR)):
         spread = jnp.broadcast_to(kinds[s:s + SR][:, None, :], band)
         own = jnp.sum(jnp.where(here, spread, 0.0), axis=-1, keepdims=True).reshape(n_tok, 1)
         hot = jnp.where(lane_level & (lane_kind == own), 1.0, 0.0).astype(BF16)
-        e = emb[s:s + SR, :cols].reshape(n_tok, -1).astype(F32) + mm(hot, table_rows)
-        emb[s:s + SR, :cols] = e.astype(BF16).reshape(SR, cols, LEV, -1)
-        if s == 0:
+        e = emb[SR + s:SR + s + SR, SC:].reshape(n_tok, -1).astype(F32) + mm(hot, table_rows)
+        emb[SR + s:SR + s + SR, SC:] = e.astype(BF16).reshape(SR, cols, LEV, -1)
+        if s == rows - SR:
             pl.semaphore_wait(barrier, len(places))
             first[0].start()
     first[1].start()
-    second = shift_up(
+    second = forward(
         fs, [((0, 3), (0, 6)), ((0, 3), (6, 12)), ((3, 6), (0, 6)), ((0, 3), (12, 24)), ((6, 12), (0, 6))],
         s2, r2,
     )
-    back = shift_down(
+    back = backward(
         fs, fine,
         [((0, 6), (18, 24)), ((9, 12), (0, 12)), ((6, 9), (18, 24)), ((9, 12), (12, 18)), ((9, 12), (18, 24))],
         rows, cols, s3, r3,
@@ -206,8 +207,8 @@
     loaded("wq", "wkv")
 
     def front(w):
-        wr, wc_ = w // 2, w % 2
-        e = emb[pl.ds(SR + WR * wr, WR), pl.ds(SC + WC * wc_, WC)].reshape(WIN, -1)
+        wr, wc_ = 1 - w // 2, 1 - w % 2
+        e = emb[pl.ds(WR * wr, WR), pl.ds(WC * wc_, WC)].reshape(WIN, -1)
         aft[...] = e
         split_tiles(nat, norm(e))
         yield
@@ -218,7 +219,7 @@
         yield
         v[...] = mm(n, wkv[:, 512:]).astype(BF16)
         yield
-        wrapped = jnp.where((lat == n_lat - 1) & (wr == 1), 2, 0)
+        wrapped = jnp.where((lat == 0) & (wr == 0), 2, 0)
         for g, levels in enumerate(GROUPS):
             at = pl.ds(g * GRP, GRP)
             for _ in attention(q.at[at], k.at[at], v.at[at], bias[wrapped + g], att, levels, 0, POS, POS):
@@ -228,7 +229,7 @@
         done[...] = a
 
     def back_half(w):
-        wr, wc_ = w // 2, w % 2
+        wr, wc_ = 1 - w // 2, 1 - w % 2
         n = norm(done[...]).astype(BF16)
         yield
         for j in range(0, 2048, 512):
@@ -236,7 +237,7 @@
             yield
         for j in range(0, 512, 256):
             f = (done[:, j:j + 256].astype(F32) + mm(hid[...], w2[:, j:j + 256])).astype(BF16)
-            fs[pl.ds(WR * wr, WR), pl.ds(WC * wc_, WC), :, j:j + 256] = f.reshape(WR, WC, LEV, -1)
+            fs[pl.ds(SR + WR * wr, WR), pl.ds(SC + WC * wc_, WC), :, j:j + 256] = f.reshape(WR, WC, LEV, -1)
             yield
 
     def window(w, carry):
@@ -283,7 +284,7 @@
     loaded("wm")
     for copy in second:
         copy.wait_recv()
-    f = fs[pl.ds(SR, rows), pl.ds(SC, cols)].reshape(rows // 2, 2, cols // 2, 2, LEV, -1)
+    f = fs[pl.ds(0, rows), pl.ds(0, cols)].reshape(rows // 2, 2, cols // 2, 2, LEV, -1)
     f = [jnp.swapaxes(f[:, j % 2, :, j // 2], 0, 1).reshape(WIN, -1) for j in range(4)]
     m = norm(jnp.concatenate(f, axis=1)).astype(BF16)
     for j in range(0, 1024, 512):
@@ -295,14 +296,14 @@
     for j in range(0, 1024, 512):
         ck[:, j:j + 512] = mm(nk, wc[:, 1024 + j:1536 + j]).astype(BF16)
         cv[:, j:j + 512] = mm(nk, wc[:, 2048 + j:2560 + j]).astype(BF16)
-    wrapped = jnp.where(lat == n_lat - 1, 4, 0)
-    third = shift_down(
+    wrapped = jnp.where(lat == 0, 4, 0)
+    third = backward(
         cs, coarse, [((3, 6), (6, 12)), ((0, 3), (6, 12)), ((3, 6), (0, 6))], WR, WC, s4, r4
     )
     keep_too = pltpu.make_async_copy(
         part(cs, (0, SR), (0, SC)), part(coarse, (SR, WR), (SC, WC)), own_sem.at[1]
     )
-    for half in (1, 0):
+    for half in (0, 1):
         nq = [by_level(cnat, levels, half * POS // 2, QPAD) for levels in GROUPS]
         nq = jnp.concatenate(nq, axis=0)
         for j in range(0, 1024, 512):
@@ -321,7 +322,7 @@
             t = (cin[at, j:j + 512].astype(F32) + mm(mixed, wco[:, j:j + 512])).astype(BF16)
             t = jnp.swapaxes(t.reshape(SC, WR, LEV, -1), 0, 1)
             cs[:, half * SC:(half + 1) * SC, :, j:j + 512] = t
-        if half == 1:
+        if half == 0:
             third[0].start()
             third[1].start()
         else:

time: 46 us -> 41.1 us (0.89)
  Pallas kernels: 43.4 us -> 38.4 us
    pallas_call x1, Pallas kernels: 43.4 us -> 38.4 us  [local(): pl.pallas_call(functools.partial(kernel, n_lat, n_lon), out_shape=(buf(ro...]
where the time goes in v7:
time: 41.1 us; the launch traced here: 40.9 us
  Pallas kernels  38.4 us (93%)
  local copies, waits for them, and re-layouts  1.83 us (4%)
  between operations  0.64 us (2%)
    pallas_call x1, Pallas kernels, local(): pl.pallas_call(functools.partial(kernel, n_lat, n_lon), out_shape=(buf(ro...  38.4 us
    unnamed x2, local copies, waits for them, and re-layouts  1.83 us

profile of v7, /device:TPU:0, one launch (start us, length us, event | category | flops | bytes accessed | tf_op | source)
XLA Modules:
  0.0 40.9 jit_solution(5333345916375373042)
XLA Ops:
  0.6 38.4 %block.1 = (bf16[12,24,4,512]{3,2,1,0:T(4,128)(2,1)S(1)}, bf16[6,12,4,1024]{3,2,1,0:T(4,128)(2,1)S(1)}) custom-call(bf16[12,24,4,512]{3,2,1,0:T(4,128)(2,1)} %x.1, s32[12,24]{1,0:T(8,128)} %kind_h.1, bf16[3,4,512]{2,1,0:T(4,128)(2,1)} %table_h.1, f32[4,144,144]{2,1,0:T(8,128)} %constant.4.clone.bias_h, f32[8,80,144]{2,1,0:T(8,128)} %constant.5.clone.cbias_h, ...), custom_call_target="tpu_custom_call" | custom-call | tf_op jit(solution)/shard_map/block/pallas_call | solution.py:350
  39.1 1.0 %copy.17 = bf16[12,24,4,512]{3,2,1,0:T(4,128)(2,1)} copy(bf16[12,24,4,512]{3,2,1,0:T(4,128)(2,1)S(1)} %get-tuple-element.2) | data formatting | bytes 2359296
  40.1 0.8 %copy.18 = bf16[6,12,4,1024]{3,2,1,0:T(4,128)(2,1)} copy(bf16[6,12,4,1024]{3,2,1,0:T(4,128)(2,1)S(1)} %get-tuple-element.3) | data formatting | bytes 1179648

commit v8 on v7

--- a/solution.py
+++ b/solution.py
@@ -35,7 +35,7 @@
         return np.where(np.stack(ok), 0.0, -1e30).astype(np.float32)
 
     full = masks(at % POS // (POS // 2))
-    coarse = masks(at % WR // SR)
+    coarse = full
     halves = np.zeros((4, 2, 2, QPAD, GRP), np.float32)
     halves[:, :, :, :POS // 2] = coarse.reshape(4, 2, 2, POS // 2, GRP).transpose(0, 2, 1, 3, 4)
     return full, halves.reshape(8, 2 * QPAD, GRP)
@@ -246,19 +246,20 @@
 
         @pl.when(w == 1)
         def _():
-            for copy in second[:3]:
+            for copy in first[2:4] + second[:3]:
                 copy.start()
             first[1].wait_recv()
 
         @pl.when(w == 2)
         def _():
             second[3].start()
+            back[0].start()
             first[0].wait_recv()
 
         @pl.when(w == 3)
         def _():
             second[4].start()
-            back[0].start()
+            back[1].start()
             for copy in first[2:]:
                 copy.wait_recv()
 
@@ -269,12 +270,10 @@
     loaded("bias", "wo")
     for _ in front(0):
         pass
-    for copy in first[2:]:
-        copy.start()
+    first[4].start()
     loaded("w1", "w2")
     load("wm", "wc", "cbias", "wco")
     lax.fori_loop(1, 4, window, 0)
-    back[1].start()
     for _ in back_half(3):
         pass
     for copy in back[2:]:
@@ -285,7 +284,7 @@
     for copy in second:
         copy.wait_recv()
     f = fs[pl.ds(0, rows), pl.ds(0, cols)].reshape(rows // 2, 2, cols // 2, 2, LEV, -1)
-    f = [jnp.swapaxes(f[:, j % 2, :, j // 2], 0, 1).reshape(WIN, -1) for j in range(4)]
+    f = [f[:, j % 2, :, j // 2].reshape(WIN, -1) for j in range(4)]
     m = norm(jnp.concatenate(f, axis=1)).astype(BF16)
     for j in range(0, 1024, 512):
         cin[:, j:j + 512] = mm(m, wm[:, j:j + 512]).astype(BF16)
@@ -298,7 +297,7 @@
         cv[:, j:j + 512] = mm(nk, wc[:, 2048 + j:2560 + j]).astype(BF16)
     wrapped = jnp.where(lat == 0, 4, 0)
     third = backward(
-        cs, coarse, [((3, 6), (6, 12)), ((0, 3), (6, 12)), ((3, 6), (0, 6))], WR, WC, s4, r4
+        cs, coarse, [((3, 6), (6, 12)), ((3, 6), (0, 6)), ((0, 3), (6, 12))], WR, WC, s4, r4
     )
     keep_too = pltpu.make_async_copy(
         part(cs, (0, SR), (0, SC)), part(coarse, (SR, WR), (SC, WC)), own_sem.at[1]
@@ -320,8 +319,7 @@
         at = slice(half * GRP, (half + 1) * GRP)
         for j in range(0, 1024, 512):
             t = (cin[at, j:j + 512].astype(F32) + mm(mixed, wco[:, j:j + 512])).astype(BF16)
-            t = jnp.swapaxes(t.reshape(SC, WR, LEV, -1), 0, 1)
-            cs[:, half * SC:(half + 1) * SC, :, j:j + 512] = t
+            cs[half * SR:(half + 1) * SR, :, :, j:j + 512] = t.reshape(SR, WC, LEV, -1)
         if half == 0:
             third[0].start()
             third[1].start()

time: 41.1 us -> 40.8 us (level)
  the two profiles are of different devices: /device:TPU:0 before, /device:TPU:7 now
where the time goes in v8:
time: 40.8 us; the launch traced here: 40.7 us
  Pallas kernels  38.2 us (94%)
  local copies, waits for them, and re-layouts  1.83 us (4%)
  between operations  0.64 us (2%)
    pallas_call x1, Pallas kernels, local(): pl.pallas_call(functools.partial(kernel, n_lat, n_lon), out_shape=(buf(ro...  38.2 us
    unnamed x2, local copies, waits for them, and re-layouts  1.83 us

profile of v8, /device:TPU:7, one launch (start us, length us, event | category | flops | bytes accessed | tf_op | source)
XLA Modules:
  0.0 40.7 jit_solution(16850221696298521176)
XLA Ops:
  0.6 38.2 %block.1 = (bf16[12,24,4,512]{3,2,1,0:T(4,128)(2,1)S(1)}, bf16[6,12,4,1024]{3,2,1,0:T(4,128)(2,1)S(1)}) custom-call(bf16[12,24,4,512]{3,2,1,0:T(4,128)(2,1)} %x.1, s32[12,24]{1,0:T(8,128)} %kind_h.1, bf16[3,4,512]{2,1,0:T(4,128)(2,1)} %table_h.1, f32[4,144,144]{2,1,0:T(8,128)} %constant.4.clone.bias_h, f32[8,80,144]{2,1,0:T(8,128)} %constant.5.clone.cbias_h, ...), custom_call_target="tpu_custom_call" | custom-call | tf_op jit(solution)/shard_map/block/pallas_call | solution.py:348
  38.8 1.0 %copy.17 = bf16[12,24,4,512]{3,2,1,0:T(4,128)(2,1)} copy(bf16[12,24,4,512]{3,2,1,0:T(4,128)(2,1)S(1)} %get-tuple-element.2) | data formatting | bytes 2359296
  39.9 0.8 %copy.18 = bf16[6,12,4,1024]{3,2,1,0:T(4,128)(2,1)} copy(bf16[6,12,4,1024]{3,2,1,0:T(4,128)(2,1)S(1)} %get-tuple-element.3) | data formatting | bytes 1179648

commit v9 on v8

--- a/solution.py
+++ b/solution.py
@@ -360,7 +360,7 @@
             buf(WIN, 4 * width),
             buf(WIN, 2 * width), buf(4 * QPAD, 2 * width), buf(WIN, 2 * width), buf(WIN, 2 * width),
             pltpu.VMEM((2 * width // LANES, WIN + LEV * (2 * QPAD - POS), LANES), F32),
-            pltpu.VMEM((2 * width // LANES, WIN, LANES), F32),
+            pltpu.VMEM((2 * width // LANES, WIN + LEV * (2 * QPAD - POS), LANES), F32),
             buf(WR, WC, lev, 2 * width),
             dma((13,)), dma((2,)), dma((5,)), dma((5,)), dma((5,)), dma((5,)), dma((5,)), dma((5,)),
             dma((3,)), dma((3,)),

time: 40.8 us -> 40.8 us (level)
  no operation moved by 1% of the time
where the time goes in v9:
time: 40.8 us; the launch traced here: 40.7 us
  Pallas kernels  38.2 us (94%)
  local copies, waits for them, and re-layouts  1.83 us (4%)
  between operations  0.64 us (2%)
    pallas_call x1, Pallas kernels, local(): pl.pallas_call(functools.partial(kernel, n_lat, n_lon), out_shape=(buf(ro...  38.2 us
    unnamed x2, local copies, waits for them, and re-layouts  1.83 us

profile of v9, /device:TPU:7, one launch (start us, length us, event | category | flops | bytes accessed | tf_op | source)
XLA Modules:
  0.0 40.7 jit_solution(17423521610605601402)
XLA Ops:
  0.6 38.2 %block.1 = (bf16[12,24,4,512]{3,2,1,0:T(4,128)(2,1)S(1)}, bf16[6,12,4,1024]{3,2,1,0:T(4,128)(2,1)S(1)}) custom-call(bf16[12,24,4,512]{3,2,1,0:T(4,128)(2,1)} %x.1, s32[12,24]{1,0:T(8,128)} %kind_h.1, bf16[3,4,512]{2,1,0:T(4,128)(2,1)} %table_h.1, f32[4,144,144]{2,1,0:T(8,128)} %constant.4.clone.bias_h, f32[8,80,144]{2,1,0:T(8,128)} %constant.5.clone.cbias_h, ...), custom_call_target="tpu_custom_call" | custom-call | tf_op jit(solution)/shard_map/block/pallas_call | solution.py:348
  38.8 1.0 %copy.17 = bf16[12,24,4,512]{3,2,1,0:T(4,128)(2,1)} copy(bf16[12,24,4,512]{3,2,1,0:T(4,128)(2,1)S(1)} %get-tuple-element.2) | data formatting | bytes 2359296
  39.9 0.8 %copy.18 = bf16[6,12,4,1024]{3,2,1,0:T(4,128)(2,1)} copy(bf16[6,12,4,1024]{3,2,1,0:T(4,128)(2,1)S(1)} %get-tuple-element.3) | data formatting | bytes 1179648
